TPU v7x, 32 devices: a whole 2x2x4 slice. The times are simulated.
32 devices in a mesh: ctx: 32 (over z, y, x, core), seq: 1.
Axes of the slice: x: 2, y: 2, z: 4, core: 2. Of those that a mesh axis runs over, the one named last changes fastest.
Arguments:
- query_states: bfloat16 [4096, 4096], P(('seq', 'ctx')), may hold values from -6.5 to 6.5
- key_states: bfloat16 [4096, 512], P(('seq', 'ctx')), may hold values from -4 to 4
- value_states: bfloat16 [4096, 512], P(('seq', 'ctx')), may hold values from -4 to 4
- block_docs: int32 [32], P('seq'), may hold values from 0 to 3, never falling along the last dimension, each value on 1 to 12 neighbouring positions
Outputs:
- attended: bfloat16 [4096, 4096], P(('seq', 'ctx'))
Inputs may be any that keep to these rules, and one draw needn't show every extreme that they name: block_docs never falls along the sequence; every document covers 1 to min(12, 16) whole blocks, and some document covers exactly that many.
All inputs are finite; a program needn't handle non-finite values.
Results may differ from a plain program's by a relative error of at most 0.004.
Values may be sent and summed in bfloat16 or wider, within the bound.
No kernel may reach another device: no remote copies, remote signals or barrier semaphores. Data moves between devices by JAX's collectives and lax.ppermute only.
A program may use at most 64 MiB of HBM per device.

v0:
```python
import functools
import math

import jax
import jax.numpy as jnp
from jax import lax
from jax.experimental import pallas as pl
from jax.experimental.pallas import tpu as pltpu
from jax.sharding import PartitionSpec as P

HD = 128
BLK = 128
NEG = -1e30
LOW, HIGH = 1e-25, 1e35
EXP2_SCALE = math.log2(math.e) / math.sqrt(HD)
OWN_UNIT, ADD_UNIT, LAST_UNIT = 8, 8, 4
F32 = jnp.float32
BF16 = jnp.bfloat16
VMEM = pl.BlockSpec(memory_space=pltpu.VMEM)
HBM = pl.BlockSpec(memory_space=pltpu.HBM)
PARAMS = pltpu.CompilerParams(vmem_limit_bytes=40 * 1024 * 1024)


def dot_nt(a, b):
    return lax.dot_general(a, b, (((1,), (1,)), ((), ())), preferred_element_type=F32)


def dot_nn(a, b):
    return lax.dot_general(a, b, (((1,), (0,)), ((), ())), preferred_element_type=F32)


def cut(index, width=HD):
    return slice(index * width, (index + 1) * width)


def with_ones(values):
    return jnp.concatenate([values, jnp.ones_like(values)], axis=1)


def unit_queries(q_ref, size, unit):
    g, first, count = unit
    return jnp.concatenate([q_ref[:, cut(g * size + first + h)] for h in range(count)], axis=0)


def unit_rows(unit):
    return slice(unit[1] * BLK, (unit[1] + unit[2]) * BLK)


def units_of(groups, size, count):
    return [(g, first, count) for g in range(groups) for first in range(0, size, count)]


def staggered(units, first, second):
    waiting = None
    for unit in units:
        ready = (unit, first(unit))
        if waiting is not None:
            second(*waiting)
        waiting = ready
    second(*waiting)


def penalty(docs_ref, position, distance):
    source = position - distance
    same = docs_ref[jnp.maximum(source, 0)] == docs_ref[position]
    return jnp.where((source >= 0) & same, 0.0, -NEG).astype(F32)


def weigh(scores, pen):
    return jnp.exp2(scores * EXP2_SCALE - pen).astype(BF16)


def causal_pen():
    row = lax.broadcasted_iota(jnp.int32, (BLK, BLK), 0)
    col = lax.broadcasted_iota(jnp.int32, (BLK, BLK), 1)
    return jnp.where(col <= row, 0.0, -NEG).astype(F32)


def own_kernel(groups, size, docs_hbm, q_hbm, k_hbm, v_hbm, weights_ref, pen_ref, q_ref, kv_ref, docs_ref, sems):
    rest = [
        pltpu.make_async_copy(k_hbm, kv_ref.at[:BLK], sems.at[groups]),
        pltpu.make_async_copy(v_hbm, kv_ref.at[BLK:], sems.at[groups + 1]),
        pltpu.make_async_copy(docs_hbm, docs_ref, sems.at[groups + 2]),
    ]
    copies = []
    for g in range(groups):
        at = cut(g, size * HD)
        copies.append(pltpu.make_async_copy(q_hbm.at[:, at], q_ref.at[:, at], sems.at[g]))
    for copy in rest[:1] + copies + rest[1:]:
        copy.start()
    pen = jnp.concatenate([causal_pen()] * OWN_UNIT, axis=0)
    rest[0].wait()
    for unit in units_of(groups, size, OWN_UNIT):
        g, rows = unit[0], unit_rows(unit)
        if unit[1] == 0:
            copies[g].wait()
        weights_ref[g, rows] = weigh(dot_nt(unit_queries(q_ref, size, unit), kv_ref[:BLK, cut(g)]), pen)
    for copy in rest[1:]:
        copy.wait()
    for i, distance in enumerate((1, 2, 3)):
        pen_ref[i] = jnp.full((8, HD), penalty(docs_ref, lax.axis_index("ctx"), distance), F32)


def weigh_all(groups, size, q_ref, pen, k_ref, weights_ref):
    for unit in units_of(groups, size, ADD_UNIT):
        scores = dot_nt(unit_queries(q_ref, size, unit), k_ref[:BLK, cut(unit[0])])
        weights_ref[unit[0], unit_rows(unit)] = weigh(scores, pen)


def weights_kernel(groups, size, distances, q_ref, pen_ref, k_ref, weights_ref):
    position = lax.axis_index("ctx")
    even, odd = (pen_ref[d - 1][:1] for d in distances)

    @pl.when(position > 1)
    def _():
        weigh_all(groups, size, q_ref, jnp.where(lax.rem(position, 2) == 1, odd, even), k_ref, weights_ref)


def add_values(unit, weights, values):
    g, rows = unit[0], unit_rows(unit)
    left = jnp.concatenate([w[g, rows] for w in weights], axis=1)
    right = jnp.concatenate([v(g) for v in values], axis=0)
    return dot_nn(left, with_ones(right))


def part(ref, first=0):
    return lambda g: ref[first : first + BLK, cut(g)]


def finish(size, unit, both, result_ref, low_high):
    total = both[:, HD:]
    result = (both[:, :HD] / total).astype(BF16)
    g, first, count = unit
    for h in range(count):
        result_ref[:, cut(g * size + first + h)] = result[cut(h, BLK)]
        if low_high[0] is not None:
            low_high[0] = jnp.minimum(low_high[0], total[cut(h, BLK)])
        low_high[1] = jnp.maximum(low_high[1], total[cut(h, BLK)])


def new_range():
    return [jnp.ones((BLK, HD), F32)] * 2


def note_range(low_high, range_ref):
    if low_high[0] is not None:
        range_ref[0] = jnp.full((8, HD), jnp.min(low_high[0]), F32)
    range_ref[1] = jnp.full((8, HD), jnp.max(low_high[1]), F32)


def early_kernel(
    groups, size, q_ref, pen_ref, own_ref, kv_ref, a_ref, beside_k, beside_v, wa_ref, weights_ref, out_hbm, range_ref,
    result_ref, sem,
):
    position = lax.axis_index("ctx")
    range_ref[...] = jnp.ones_like(range_ref)

    @pl.when(position > 1)
    def _():
        weigh_all(groups, size, q_ref, pen_ref[1][:1], a_ref, wa_ref)

    @pl.when(lax.rem(position, 2) == 1)
    def _():
        weigh_all(groups, size, q_ref, pen_ref[0][:1], beside_k, weights_ref)

    def store_all(weights, values):
        low_high = new_range()
        for unit in units_of(groups, size, size):
            finish(size, unit, add_values(unit, weights, values), result_ref, low_high)
        note_range(low_high, range_ref)
        copy = pltpu.make_async_copy(result_ref, out_hbm, sem)
        copy.start()
        copy.wait()

    @pl.when(position == 0)
    def _():
        store_all([own_ref], [part(kv_ref, BLK)])

    @pl.when(position == 1)
    def _():
        store_all([own_ref, weights_ref], [part(kv_ref, BLK), part(beside_v)])


def values_kernel(
    groups, size, own_ref, wa_ref, wb_ref, ws_ref, kv_ref, va_ref, vb_ref, vs_ref, early_range, both_ref, range_ref,
):
    position = lax.axis_index("ctx")
    odd = lax.rem(position, 2) == 1
    range_ref[...] = early_range[...]

    def whole(weights, values):
        low = jnp.ones((BLK, HD), F32)
        for unit in units_of(groups, size, ADD_UNIT):
            both = add_values(unit, weights, values)
            both_ref[unit[0], unit_rows(unit)] = both
            for h in range(unit[2]):
                low = jnp.minimum(low, both[cut(h, BLK), HD:])
        range_ref[0] = jnp.full((8, HD), jnp.min(low), F32)

    weights = [own_ref, wa_ref, wb_ref]
    values = [part(kv_ref, BLK), part(va_ref), part(vb_ref)]

    @pl.when(jnp.logical_not(odd) & (position > 1))
    def _():
        whole(weights, values)

    @pl.when(odd & (position > 1))
    def _():
        whole(weights + [ws_ref], values + [part(vs_ref)])


def last_kernel(
    groups, size, q_ref, pen_ref, both_ref, c_ref, own_ref, wa_ref, wb_ref, ws_ref, kv_ref, ak_ref, av_ref, bk_ref, bv_ref, sk_ref, sv_ref, early_range, _, out_hbm, result_ref, range_ref, sems,
):
    position = lax.axis_index("ctx")
    odd = lax.rem(position, 2) == 1
    units = units_of(groups, size, LAST_UNIT)
    copies = {}
    for n, unit in enumerate(units):
        start = (unit[0] * size + unit[1]) * HD
        at = slice(start, start + unit[2] * HD)
        copies[unit] = pltpu.make_async_copy(result_ref.at[:, at], out_hbm.at[:, at], sems.at[n])
    range_ref[...] = early_range[...]

    @pl.when(jnp.logical_not(odd) & (position > 1))
    def _():
        low_high = [None, new_range()[1]]
        pen = pen_ref[2][:1]

        def first(unit):
            return weigh(dot_nt(unit_queries(q_ref, size, unit), c_ref[:BLK, cut(unit[0])]), pen)

        def second(unit, weights):
            values = with_ones(c_ref[BLK:, cut(unit[0])])
            both = both_ref[unit[0], unit_rows(unit)] + dot_nn(weights, values)
            finish(size, unit, both, result_ref, low_high)
            copies[unit].start()

        staggered(units, first, second)
        note_range(low_high, range_ref)

    @pl.when(odd & (position > 1))
    def _():
        low_high = [None, new_range()[1]]
        for unit in units:
            finish(size, unit, both_ref[unit[0], unit_rows(unit)], result_ref, low_high)
            copies[unit].start()
        note_range(low_high, range_ref)

    safe = (jnp.min(range_ref[0]) > LOW) & (jnp.max(range_ref[1]) < HIGH)

    @pl.when(position > 1)
    def _():
        for copy in copies.values():
            copy.wait()

    @pl.when(jnp.logical_not(safe))
    def _():
        pens = [causal_pen()] + [pen_ref[i][:1] for i in range(3)]
        pairs = (((bk_ref, bv_ref, 0), (sk_ref, sv_ref, 0)), ((ak_ref, av_ref, 0),) * 2, ((c_ref, c_ref, BLK), (bk_ref, bv_ref, 0)))
        for g in range(groups):
            keys = [kv_ref[:BLK, cut(g)]]
            values = [kv_ref[BLK:, cut(g)]]
            for (ek, ev, first), (ok, ov, _) in pairs:
                keys.append(jnp.where(odd, ok[:BLK, cut(g)], ek[:BLK, cut(g)]))
                values.append(jnp.where(odd, ov[:BLK, cut(g)], ev[first : first + BLK, cut(g)]))

            def one_head(h, _):
                at = pl.ds(pl.multiple_of((g * size + h) * HD, HD), HD)
                queries = q_ref[:, at]
                scores = [dot_nt(queries, x) - pen for x, pen in zip(keys, pens)]
                top = functools.reduce(jnp.maximum, [jnp.max(x, axis=1, keepdims=True) for x in scores])
                weights = [jnp.exp2((x - top) * EXP2_SCALE) for x in scores]
                total = sum(jnp.sum(w, axis=1, keepdims=True) for w in weights)
                product = sum(dot_nn(w.astype(BF16), x) for w, x in zip(weights, values))
                result_ref[:, at] = (product / total).astype(BF16)
                return 0

            lax.fori_loop(0, size, one_head, 0)
        store = pltpu.make_async_copy(result_ref, out_hbm, sems.at[0])
        store.start()
        store.wait()


def routes(n):
    step = n // 4
    ring = [(i, (i + 2) % n) for i in range(n)]
    across = {i: i + 3 for i in range(1, n - 3, 2)}
    first = [n - 3 - step * k for k in (1, 2, 3)] + [2]
    second = [n - 5 - step * k for k in (0, 1, 2)] + [step + 1, 0]
    for at, places in ((n - 3, first), (n - 1, second)):
        for place in places:
            across[at] = place
            at = place - 1
    across.update({i: i + 1 for i in range(0, n, 2) if i not in across})
    swap = [(i, i ^ 1) for i in range(n)]
    return ring, sorted(across.items()), swap


def in_hbm(array):
    return pltpu.with_memory_space_constraint(array, pltpu.HBM)


def after(value, *others):
    return lax.optimization_barrier((value, *others))[0]


def on_device(queries, keys, values, docs):
    row_count, width = keys.shape
    groups = width // HD
    size = queries.shape[1] // width
    rows = size * BLK
    n = lax.axis_size("ctx")
    assert row_count == BLK and n % 16 == 0
    ring, across, swap = routes(n)
    cost = pl.CostEstimate(flops=0, bytes_accessed=0, transcendentals=0)
    weights_shape = jax.ShapeDtypeStruct((groups, rows, HD), BF16)
    both_shape = jax.ShapeDtypeStruct((groups, rows, 2 * HD), F32)
    pack_shape = jax.ShapeDtypeStruct((2 * BLK, width), BF16)
    range_shape = jax.ShapeDtypeStruct((2, 8, HD), F32)
    result = jax.ShapeDtypeStruct(queries.shape, BF16)
    dma = pltpu.SemaphoreType.DMA

    def call(kernel, name, out_shape, operands, out_specs=None, in_specs=None, scratch_shapes=(), **options):
        many = isinstance(out_shape, tuple)
        return pl.pallas_call(
            kernel,
            out_shape=out_shape,
            in_specs=in_specs or [VMEM] * len(operands),
            out_specs=out_specs or ((VMEM,) * len(out_shape) if many else VMEM),
            scratch_shapes=scratch_shapes,
            compiler_params=PARAMS,
            cost_estimate=cost,
            name=name,
            **options,
        )(*operands)

    def move(block, route):
        return lax.ppermute(block, "ctx", route)

    def own():
        return call(
            functools.partial(own_kernel, groups, size), "own_block",
            (weights_shape, jax.ShapeDtypeStruct((3, 8, HD), F32), result, pack_shape),
            [in_hbm(x) for x in (docs, queries, keys, values)], in_specs=[HBM] * 4,
            scratch_shapes=[pltpu.SMEM(docs.shape, jnp.int32), dma((groups + 3,))],
        )

    def early(*operands):
        return call(
            functools.partial(early_kernel, groups, size), "early_rows",
            (weights_shape, weights_shape, result, range_shape), operands, out_specs=(VMEM, VMEM, HBM, VMEM),
            scratch_shapes=[pltpu.VMEM(result.shape, BF16), dma(())],
        )

    def weigh_block(name, distances, *operands):
        return call(functools.partial(weights_kernel, groups, size, distances), name, weights_shape, operands)

    ak, av = move(keys, ring), move(values, ring)
    sk, sv = move(keys, swap), move(values, swap)
    w_own, pen, local, block = own()
    block_c = move(after(block, pen), across)
    w_a, w_s, stored, early_range = early(local, pen, w_own, block, ak, sk, sv)
    bk = move(after(ak, pen), swap)
    bv = move(after(av, w_a), swap)
    w_b = weigh_block("third_weights", (1, 3), local, pen, bk)
    both, early_range = call(
        functools.partial(values_kernel, groups, size), "values", (both_shape, range_shape),
        (w_own, w_a, w_b, w_s, block, av, bv, sv, early_range),
    )
    operands = (local, pen, both, block_c, w_own, w_a, w_b, w_s, block, ak, av, bk, bv, sk, sv, early_range, in_hbm(stored))
    return call(
        functools.partial(last_kernel, groups, size), "last_blocks", result, operands,
        in_specs=[VMEM] * 16 + [HBM], out_specs=HBM, input_output_aliases={16: 0},
        scratch_shapes=[pltpu.VMEM(result.shape, BF16), pltpu.VMEM(range_shape.shape, F32), dma((groups * size // LAST_UNIT,))],
    )


def solution(mesh):
    return jax.shard_map(
        on_device,
        mesh=mesh,
        in_specs=(
            P(("seq", "ctx"), None),
            P(("seq", "ctx"), None),
            P(("seq", "ctx"), None),
            P("seq"),
        ),
        out_specs=P(("seq", "ctx"), None),
        check_vma=False,
    )
```

profile of v0, /device:TPU:1, one launch (start us, length us, event | category | flops | bytes accessed | tf_op | source)
XLA Modules:
  0.0 32.8 jit_solution(17193269986389680334)
XLA Ops:
  0.0 2.0 %collective-permute-start = (bf16[128,512]{1,0:T(8,128)(2,1)}, bf16[128,512]{1,0:T(8,128)(2,1)S(1)}, u32[]{:S(2)}, u32[]{:S(2)}) collective-permute-start(bf16[128,512]{1,0:T(8,128)(2,1)} %k_hbm.1), channel_id=1, source_target_pairs={{0,2},{1,3},{2,4},{3,5},{4,6},{5,7},{6,8},{7,9},{8,10},{9,11},{10,... | collective-permute-start | bytes 393224 | tf_op jit(solution)/shard_map/ppermute | solution.py:339
  2.0 1.0 %collective-permute-start.1 = (bf16[128,512]{1,0:T(8,128)(2,1)}, bf16[128,512]{1,0:T(8,128)(2,1)S(1)}, u32[]{:S(2)}, u32[]{:S(2)}) collective-permute-start(bf16[128,512]{1,0:T(8,128)(2,1)} %k_hbm.1), channel_id=1, source_target_pairs={{0,1},{1,0},{2,3},{3,2},{4,5},{5,4},{6,7},{7,6},{8,9},{9,8},{10,11... | collective-permute-start | bytes 393224 | tf_op jit(solution)/shard_map/ppermute | solution.py:339
  3.0 0.0 collective-permute-start.2
  3.0 1.2 %collective-permute-start.4 = (bf16[128,512]{1,0:T(8,128)(2,1)}, bf16[128,512]{1,0:T(8,128)(2,1)S(1)}, u32[]{:S(2)}, u32[]{:S(2)}) collective-permute-start(bf16[128,512]{1,0:T(8,128)(2,1)} %v_hbm.1), channel_id=1, source_target_pairs={{0,2},{1,3},{2,4},{3,5},{4,6},{5,7},{6,8},{7,9},{8,10},{9,11},{10,... | collective-permute-start | bytes 393224 | tf_op jit(solution)/shard_map/ppermute | solution.py:339
  4.2 2.3 %own_block.1 = (bf16[4,1024,128]{2,1,0:T(8,128)(2,1)S(1)}, f32[3,8,128]{2,1,0:T(8,128)S(1)}, bf16[128,4096]{1,0:T(8,128)(2,1)S(1)}, bf16[256,512]{1,0:T(8,128)(2,1)S(1)}) custom-call(s32[32]{0:T(128)} %docs_hbm.1, bf16[128,4096]{1,0:T(8,128)(2,1)} %q_hbm.1, bf16[128,512]{1,0:T(8,128)(2,1)} %k_hbm.1, bf16[128,512]{1,0:T(8,128)(2,1)} %v_hbm.1), custom_call_target="tpu_custom_call" | custom-call | tf_op jit(solution)/shard_map/own_block/pallas_call | solution.py:326
  6.5 2.0 %collective-permute-start.6 = (bf16[256,512]{1,0:T(8,128)(2,1)S(1)}, bf16[256,512]{1,0:T(8,128)(2,1)S(1)}, u32[]{:S(2)}, u32[]{:S(2)}) collective-permute-start(bf16[256,512]{1,0:T(8,128)(2,1)S(1)} %get-tuple-element.28.kv_ref), channel_id=1, source_target_pairs={{0,1},{1,4},{2,3},{3,6},{4,2},{5,8},{6,7},{7,10},{8,0},{9,12},{10,... | collective-permute-start | bytes 786440 | tf_op jit(solution)/shard_map/ppermute | solution.py:339
  8.5 1.0 %collective-permute-done.a_ref.ak_ref = bf16[128,512]{1,0:T(8,128)(2,1)S(1)} collective-permute-done((bf16[128,512]{1,0:T(8,128)(2,1)}, bf16[128,512]{1,0:T(8,128)(2,1)S(1)}, u32[]{:S(2)}, u32[]{:S(2)}) %collective-permute-start) | collective-permute-done | bytes 131104 | tf_op jit(solution)/shard_map/ppermute | solution.py:339
  9.5 2.0 %collective-permute-start.3 = (bf16[128,512]{1,0:T(8,128)(2,1)S(1)}, bf16[128,512]{1,0:T(8,128)(2,1)S(1)}, u32[]{:S(2)}, u32[]{:S(2)}) collective-permute-start(bf16[128,512]{1,0:T(8,128)(2,1)S(1)} %collective-permute-done.a_ref.ak_ref), channel_id=1, source_target_pairs={{0,1},{1,0},{2,3},{3,2},{4,5},{5,4},{6,7},{7,6},{8,9},{9,8},{10,11... | collective-permute-start | bytes 393224 | tf_op jit(solution)/shard_map/ppermute | solution.py:339
  11.5 0.0 collective-permute-done.1.beside_k.sk_ref
  11.5 0.0 collective-permute-done.2.beside_v.vs_ref.sv_ref
  11.5 2.2 %early_rows.1 = (bf16[4,1024,128]{2,1,0:T(8,128)(2,1)S(1)}, bf16[4,1024,128]{2,1,0:T(8,128)(2,1)S(1)}, bf16[128,4096]{1,0:T(8,128)(2,1)}, f32[2,8,128]{2,1,0:T(8,128)S(1)}) custom-call(bf16[128,4096]{1,0:T(8,128)(2,1)S(1)} %get-tuple-element.18.q_ref, f32[3,8,128]{2,1,0:T(8,128)S(1)} %get-tuple-element.19.pen_ref, ...), custom_call_target="tpu_custom_call" | custom-call | tf_op jit(solution)/shard_map/early_rows/pallas_call | solution.py:326
  13.7 0.0 collective-permute-done.4.va_ref.av_ref
  13.7 0.1 collective-permute-start.5
  13.8 0.0 collective-permute-done.3.k_ref.bk_ref
  13.8 1.3 %collective-permute-done.5.vb_ref.bv_ref = bf16[128,512]{1,0:T(8,128)(2,1)S(1)} collective-permute-done((bf16[128,512]{1,0:T(8,128)(2,1)S(1)}, bf16[128,512]{1,0:T(8,128)(2,1)S(1)}, u32[]{:S(2)}, u32[]{:S(2)}) %collective-permute-start.5) | collective-permute-done | bytes 131104 | tf_op jit(solution)/shard_map/ppermute | solution.py:339
  15.1 0.0 collective-permute-done.6.c_ref
  15.1 17.7 %last_blocks.1 = bf16[128,4096]{1,0:T(8,128)(2,1)} custom-call(bf16[128,4096]{1,0:T(8,128)(2,1)S(1)} %get-tuple-element.18.q_ref, f32[3,8,128]{2,1,0:T(8,128)S(1)} %get-tuple-element.19.pen_ref, f32[4,1024,256]{2,1,0:T(8,128)S(1)} %get-tuple-element.27.both_ref, bf16[256,512]{1,0:T(8,128)(2,1)S(1)} %collective-permute-done.6.c_ref, ...), custom_call_target="tpu_custom_call", output_to_operand_aliasing={{}: (16, {})} | custom-call | tf_op jit(solution)/shard_map/last_blocks/pallas_call | solution.py:326
  (2 shorter events, 0.0 us)
Async XLA Ops:
  0.0 9.5 %collective-permute-start = (bf16[128,512]{1,0:T(8,128)(2,1)}, bf16[128,512]{1,0:T(8,128)(2,1)S(1)}, u32[]{:S(2)}, u32[]{:S(2)}) collective-permute-start(bf16[128,512]{1,0:T(8,128)(2,1)} %k_hbm.1), channel_id=1, source_target_pairs={{0,2},{1,3},{2,4},{3,5},{4,6},{5,7},{6,8},{7,9},{8,10},{9,11},{10,... | collective-permute-start | bytes 393224 | tf_op jit(solution)/shard_map/ppermute | solution.py:339
  2.0 9.4 %collective-permute-start.1 = (bf16[128,512]{1,0:T(8,128)(2,1)}, bf16[128,512]{1,0:T(8,128)(2,1)S(1)}, u32[]{:S(2)}, u32[]{:S(2)}) collective-permute-start(bf16[128,512]{1,0:T(8,128)(2,1)} %k_hbm.1), channel_id=1, source_target_pairs={{0,1},{1,0},{2,3},{3,2},{4,5},{5,4},{6,7},{7,6},{8,9},{9,8},{10,11... | collective-permute-start | bytes 393224 | tf_op jit(solution)/shard_map/ppermute | solution.py:339
  3.0 8.5 %collective-permute-start.2 = (bf16[128,512]{1,0:T(8,128)(2,1)}, bf16[128,512]{1,0:T(8,128)(2,1)S(1)}, u32[]{:S(2)}, u32[]{:S(2)}) collective-permute-start(bf16[128,512]{1,0:T(8,128)(2,1)} %v_hbm.1), channel_id=1, source_target_pairs={{0,1},{1,0},{2,3},{3,2},{4,5},{5,4},{6,7},{7,6},{8,9},{9,8},{10,11... | collective-permute-start | bytes 393224 | tf_op jit(solution)/shard_map/ppermute | solution.py:339
  3.0 10.7 %collective-permute-start.4 = (bf16[128,512]{1,0:T(8,128)(2,1)}, bf16[128,512]{1,0:T(8,128)(2,1)S(1)}, u32[]{:S(2)}, u32[]{:S(2)}) collective-permute-start(bf16[128,512]{1,0:T(8,128)(2,1)} %v_hbm.1), channel_id=1, source_target_pairs={{0,2},{1,3},{2,4},{3,5},{4,6},{5,7},{6,8},{7,9},{8,10},{9,11},{10,... | collective-permute-start | bytes 393224 | tf_op jit(solution)/shard_map/ppermute | solution.py:339
  6.5 8.6 %collective-permute-start.6 = (bf16[256,512]{1,0:T(8,128)(2,1)S(1)}, bf16[256,512]{1,0:T(8,128)(2,1)S(1)}, u32[]{:S(2)}, u32[]{:S(2)}) collective-permute-start(bf16[256,512]{1,0:T(8,128)(2,1)S(1)} %get-tuple-element.28.kv_ref), channel_id=1, source_target_pairs={{0,1},{1,4},{2,3},{3,6},{4,2},{5,8},{6,7},{7,10},{8,0},{9,12},{10,... | collective-permute-start | bytes 786440 | tf_op jit(solution)/shard_map/ppermute | solution.py:339
  9.5 4.3 %collective-permute-start.3 = (bf16[128,512]{1,0:T(8,128)(2,1)S(1)}, bf16[128,512]{1,0:T(8,128)(2,1)S(1)}, u32[]{:S(2)}, u32[]{:S(2)}) collective-permute-start(bf16[128,512]{1,0:T(8,128)(2,1)S(1)} %collective-permute-done.a_ref.ak_ref), channel_id=1, source_target_pairs={{0,1},{1,0},{2,3},{3,2},{4,5},{5,4},{6,7},{7,6},{8,9},{9,8},{10,11... | collective-permute-start | bytes 393224 | tf_op jit(solution)/shard_map/ppermute | solution.py:339
  13.7 1.4 %collective-permute-start.5 = (bf16[128,512]{1,0:T(8,128)(2,1)S(1)}, bf16[128,512]{1,0:T(8,128)(2,1)S(1)}, u32[]{:S(2)}, u32[]{:S(2)}) collective-permute-start(bf16[128,512]{1,0:T(8,128)(2,1)S(1)} %collective-permute-done.4.va_ref.av_ref), channel_id=1, source_target_pairs={{0,1},{1,0},{2,3},{3,2},{4,5},{5,4},{6,7},{7,6},{8,9},{9,8},{10,11... | collective-permute-start | bytes 393224 | tf_op jit(solution)/shard_map/ppermute | solution.py:339
where the time goes:
time: 33 us; the launch traced here: 32.8 us
  Pallas kernels  22.2 us (67%)
  starting transfers between devices  8.24 us (25%)
  waiting for transfers between devices  2.3 us (7%)
    pallas_call x5, Pallas kernels, call(): pl.pallas_call(kernel, out_shape=out_shape, in_specs=in_specs or [VMEM] *...  22.2 us
    ppermute x7, starting transfers between devices, move(): return lax.ppermute(block, 'ctx', route)  8.24 us
    ppermute x7, waiting for transfers between devices, move(): return lax.ppermute(block, 'ctx', route)  2.3 us
  transfers between devices with their start and end apart: 7, of which 2 were waited for; matrix products, arithmetic and copies ran while one was open for 0% of the time, Pallas kernels for 14%

commit v1 on v0

--- a/solution.py
+++ b/solution.py
@@ -13,7 +13,7 @@
 NEG = -1e30
 LOW, HIGH = 1e-25, 1e35
 EXP2_SCALE = math.log2(math.e) / math.sqrt(HD)
-OWN_UNIT, ADD_UNIT, LAST_UNIT = 8, 8, 4
+OWN_UNIT, ADD_UNIT, LAST_UNIT = 4, 8, 8
 F32 = jnp.float32
 BF16 = jnp.bfloat16
 VMEM = pl.BlockSpec(memory_space=pltpu.VMEM)
@@ -107,13 +107,19 @@
         weights_ref[unit[0], unit_rows(unit)] = weigh(scores, pen)
 
 
-def weights_kernel(groups, size, distances, q_ref, pen_ref, k_ref, weights_ref):
+def weights_kernel(groups, size, distances, q_ref, pen_ref, k_ref, rows_ref, weights_ref, out_hbm, sem):
     position = lax.axis_index("ctx")
     even, odd = (pen_ref[d - 1][:1] for d in distances)
 
     @pl.when(position > 1)
     def _():
         weigh_all(groups, size, q_ref, jnp.where(lax.rem(position, 2) == 1, odd, even), k_ref, weights_ref)
+
+    @pl.when(position <= 1)
+    def _():
+        copy = pltpu.make_async_copy(rows_ref, out_hbm, sem)
+        copy.start()
+        copy.wait()
 
 
 def add_values(unit, weights, values):
@@ -149,8 +155,7 @@
 
 
 def early_kernel(
-    groups, size, q_ref, pen_ref, own_ref, kv_ref, a_ref, beside_k, beside_v, wa_ref, weights_ref, out_hbm, range_ref,
-    result_ref, sem,
+    groups, size, q_ref, pen_ref, own_ref, kv_ref, a_ref, beside_k, beside_v, wa_ref, weights_ref, result_ref, range_ref,
 ):
     position = lax.axis_index("ctx")
     range_ref[...] = jnp.ones_like(range_ref)
@@ -168,9 +173,6 @@
         for unit in units_of(groups, size, size):
             finish(size, unit, add_values(unit, weights, values), result_ref, low_high)
         note_range(low_high, range_ref)
-        copy = pltpu.make_async_copy(result_ref, out_hbm, sem)
-        copy.start()
-        copy.wait()
 
     @pl.when(position == 0)
     def _():
@@ -182,7 +184,7 @@
 
 
 def values_kernel(
-    groups, size, own_ref, wa_ref, wb_ref, ws_ref, kv_ref, va_ref, vb_ref, vs_ref, early_range, both_ref, range_ref,
+    groups, size, own_ref, wa_ref, ws_ref, kv_ref, va_ref, vs_ref, early_range, both_ref, range_ref,
 ):
     position = lax.axis_index("ctx")
     odd = lax.rem(position, 2) == 1
@@ -197,8 +199,8 @@
                 low = jnp.minimum(low, both[cut(h, BLK), HD:])
         range_ref[0] = jnp.full((8, HD), jnp.min(low), F32)
 
-    weights = [own_ref, wa_ref, wb_ref]
-    values = [part(kv_ref, BLK), part(va_ref), part(vb_ref)]
+    weights = [own_ref, wa_ref]
+    values = [part(kv_ref, BLK), part(va_ref)]
 
     @pl.when(jnp.logical_not(odd) & (position > 1))
     def _():
@@ -209,20 +211,45 @@
         whole(weights + [ws_ref], values + [part(vs_ref)])
 
 
-def last_kernel(
-    groups, size, q_ref, pen_ref, both_ref, c_ref, own_ref, wa_ref, wb_ref, ws_ref, kv_ref, ak_ref, av_ref, bk_ref, bv_ref, sk_ref, sv_ref, early_range, _, out_hbm, result_ref, range_ref, sems,
-):
-    position = lax.axis_index("ctx")
-    odd = lax.rem(position, 2) == 1
-    units = units_of(groups, size, LAST_UNIT)
+def out_copies(units, size, result_ref, out_hbm, sems):
     copies = {}
     for n, unit in enumerate(units):
         start = (unit[0] * size + unit[1]) * HD
         at = slice(start, start + unit[2] * HD)
         copies[unit] = pltpu.make_async_copy(result_ref.at[:, at], out_hbm.at[:, at], sems.at[n])
-    range_ref[...] = early_range[...]
-
-    @pl.when(jnp.logical_not(odd) & (position > 1))
+    return copies
+
+
+def odd_kernel(groups, size, both_ref, wb_ref, bv_ref, so_far, _, out_hbm, range_ref, result_ref, sems):
+    position = lax.axis_index("ctx")
+    range_ref[...] = so_far[...]
+
+    @pl.when((lax.rem(position, 2) == 1) & (position > 1))
+    def _():
+        units = units_of(groups, size, LAST_UNIT)
+        copies = out_copies(units, size, result_ref, out_hbm, sems)
+        low_high = [None, new_range()[1]]
+        for unit in units:
+            both = both_ref[unit[0], unit_rows(unit)] + add_values(unit, [wb_ref], [part(bv_ref)])
+            finish(size, unit, both, result_ref, low_high)
+            copies[unit].start()
+        note_range(low_high, range_ref)
+        for copy in copies.values():
+            copy.wait()
+
+
+def last_kernel(
+    groups, size, q_ref, pen_ref, both_ref, c_ref, own_ref, wa_ref, wb_ref, ws_ref, kv_ref,
+    ak_ref, av_ref, bk_ref, bv_ref, sk_ref, sv_ref, so_far, _, out_hbm, result_ref, range_ref, sems,
+):
+    position = lax.axis_index("ctx")
+    odd = lax.rem(position, 2) == 1
+    units = units_of(groups, size, LAST_UNIT)
+    copies = out_copies(units, size, result_ref, out_hbm, sems)
+    range_ref[...] = so_far[...]
+    waits = jnp.logical_not(odd) & (position > 1)
+
+    @pl.when(waits)
     def _():
         low_high = [None, new_range()[1]]
         pen = pen_ref[2][:1]
@@ -231,25 +258,19 @@
             return weigh(dot_nt(unit_queries(q_ref, size, unit), c_ref[:BLK, cut(unit[0])]), pen)
 
         def second(unit, weights):
-            values = with_ones(c_ref[BLK:, cut(unit[0])])
-            both = both_ref[unit[0], unit_rows(unit)] + dot_nn(weights, values)
+            g, at = unit[0], unit_rows(unit)
+            weights = jnp.concatenate([wb_ref[g, at], weights], axis=1)
+            values = jnp.concatenate([bv_ref[:, cut(g)], c_ref[BLK:, cut(g)]], axis=0)
+            both = both_ref[g, at] + dot_nn(weights, with_ones(values))
             finish(size, unit, both, result_ref, low_high)
             copies[unit].start()
 
         staggered(units, first, second)
         note_range(low_high, range_ref)
 
-    @pl.when(odd & (position > 1))
-    def _():
-        low_high = [None, new_range()[1]]
-        for unit in units:
-            finish(size, unit, both_ref[unit[0], unit_rows(unit)], result_ref, low_high)
-            copies[unit].start()
-        note_range(low_high, range_ref)
-
     safe = (jnp.min(range_ref[0]) > LOW) & (jnp.max(range_ref[1]) < HIGH)
 
-    @pl.when(position > 1)
+    @pl.when(waits)
     def _():
         for copy in copies.values():
             copy.wait()
@@ -349,30 +370,38 @@
     def early(*operands):
         return call(
             functools.partial(early_kernel, groups, size), "early_rows",
-            (weights_shape, weights_shape, result, range_shape), operands, out_specs=(VMEM, VMEM, HBM, VMEM),
-            scratch_shapes=[pltpu.VMEM(result.shape, BF16), dma(())],
+            (weights_shape, weights_shape, result, range_shape), operands,
         )
 
     def weigh_block(name, distances, *operands):
-        return call(functools.partial(weights_kernel, groups, size, distances), name, weights_shape, operands)
+        return call(
+            functools.partial(weights_kernel, groups, size, distances), name, (weights_shape, result), operands,
+            out_specs=(VMEM, HBM), scratch_shapes=[dma(())],
+        )
 
     ak, av = move(keys, ring), move(values, ring)
     sk, sv = move(keys, swap), move(values, swap)
     w_own, pen, local, block = own()
     block_c = move(after(block, pen), across)
-    w_a, w_s, stored, early_range = early(local, pen, w_own, block, ak, sk, sv)
+    w_a, w_s, first_rows, early_range = early(local, pen, w_own, block, ak, sk, sv)
     bk = move(after(ak, pen), swap)
     bv = move(after(av, w_a), swap)
-    w_b = weigh_block("third_weights", (1, 3), local, pen, bk)
+    w_b, stored = weigh_block("third_weights", (1, 3), local, pen, bk, first_rows)
     both, early_range = call(
         functools.partial(values_kernel, groups, size), "values", (both_shape, range_shape),
-        (w_own, w_a, w_b, w_s, block, av, bv, sv, early_range),
+        (w_own, w_a, w_s, block, av, sv, early_range),
     )
-    operands = (local, pen, both, block_c, w_own, w_a, w_b, w_s, block, ak, av, bk, bv, sk, sv, early_range, in_hbm(stored))
+    unit_sems = dma((groups * size // LAST_UNIT,))
+    stored, so_far = call(
+        functools.partial(odd_kernel, groups, size), "odd_rows", (result, range_shape), (both, w_b, bv, early_range, in_hbm(stored)),
+        in_specs=[VMEM] * 4 + [HBM], out_specs=(HBM, VMEM), input_output_aliases={4: 0},
+        scratch_shapes=[pltpu.VMEM(result.shape, BF16), unit_sems],
+    )
+    operands = (local, pen, both, block_c, w_own, w_a, w_b, w_s, block, ak, av, bk, bv, sk, sv, so_far, in_hbm(stored))
     return call(
         functools.partial(last_kernel, groups, size), "last_blocks", result, operands,
         in_specs=[VMEM] * 16 + [HBM], out_specs=HBM, input_output_aliases={16: 0},
-        scratch_shapes=[pltpu.VMEM(result.shape, BF16), pltpu.VMEM(range_shape.shape, F32), dma((groups * size // LAST_UNIT,))],
+        scratch_shapes=[pltpu.VMEM(result.shape, BF16), pltpu.VMEM(range_shape.shape, F32), unit_sems],
     )
 
 

time: 33 us -> 32.7 us (level)
  waiting for transfers between devices: 2.3 us -> 1.21 us
  starting transfers between devices: 8.24 us -> 8.9 us
    ppermute x7, waiting for transfers between devices: 2.3 us -> 1.21 us  [move(): return lax.ppermute(block, 'ctx', route)]
    ppermute x7, starting transfers between devices: 8.24 us -> 8.9 us  [move(): return lax.ppermute(block, 'ctx', route)]
    pallas_call x5 -> x6, Pallas kernels: 22.2 us -> 22.1 us  [call(): pl.pallas_call(kernel, out_shape=out_shape, in_specs=in_specs or [VMEM] *...]
  transfers between devices with their start and end apart: 7 -> 7, of which waited for: 2 -> 1; matrix products, arithmetic and copies ran while one was open for 0% -> 0% of each run, Pallas kernels for 14% -> 14%
where the time goes in v1:
time: 32.7 us; the launch traced here: 32.3 us
  Pallas kernels  22.1 us (68%)
  starting transfers between devices  8.9 us (27%)
  waiting for transfers between devices  1.21 us (4%)
    pallas_call x6, Pallas kernels, call(): pl.pallas_call(kernel, out_shape=out_shape, in_specs=in_specs or [VMEM] *...  22.1 us
    ppermute x7, starting transfers between devices, move(): return lax.ppermute(block, 'ctx', route)  8.9 us
    ppermute x7, waiting for transfers between devices, move(): return lax.ppermute(block, 'ctx', route)  1.21 us
  transfers between devices with their start and end apart: 7, of which 1 were waited for; matrix products, arithmetic and copies ran while one was open for 0% of the time, Pallas kernels for 14%

profile of v1, /device:TPU:1, one launch (start us, length us, event | category | flops | bytes accessed | tf_op | source)
XLA Modules:
  0.0 32.3 jit_solution(4151936324274166681)
XLA Ops:
  0.0 2.0 %collective-permute-start = (bf16[128,512]{1,0:T(8,128)(2,1)}, bf16[128,512]{1,0:T(8,128)(2,1)S(1)}, u32[]{:S(2)}, u32[]{:S(2)}) collective-permute-start(bf16[128,512]{1,0:T(8,128)(2,1)} %k_hbm.1), channel_id=1, source_target_pairs={{0,2},{1,3},{2,4},{3,5},{4,6},{5,7},{6,8},{7,9},{8,10},{9,11},{10,... | collective-permute-start | bytes 393224 | tf_op jit(solution)/shard_map/ppermute | solution.py:360
  2.0 1.0 %collective-permute-start.2 = (bf16[128,512]{1,0:T(8,128)(2,1)}, bf16[128,512]{1,0:T(8,128)(2,1)S(1)}, u32[]{:S(2)}, u32[]{:S(2)}) collective-permute-start(bf16[128,512]{1,0:T(8,128)(2,1)} %v_hbm.1), channel_id=1, source_target_pairs={{0,1},{1,0},{2,3},{3,2},{4,5},{5,4},{6,7},{7,6},{8,9},{9,8},{10,11... | collective-permute-start | bytes 393224 | tf_op jit(solution)/shard_map/ppermute | solution.py:360
  3.0 0.0 collective-permute-start.1
  3.0 1.2 %collective-permute-start.3 = (bf16[128,512]{1,0:T(8,128)(2,1)}, bf16[128,512]{1,0:T(8,128)(2,1)S(1)}, u32[]{:S(2)}, u32[]{:S(2)}) collective-permute-start(bf16[128,512]{1,0:T(8,128)(2,1)} %v_hbm.1), channel_id=1, source_target_pairs={{0,2},{1,3},{2,4},{3,5},{4,6},{5,7},{6,8},{7,9},{8,10},{9,11},{10,... | collective-permute-start | bytes 393224 | tf_op jit(solution)/shard_map/ppermute | solution.py:360
  4.2 2.1 %own_block.1 = (bf16[4,1024,128]{2,1,0:T(8,128)(2,1)S(1)}, f32[3,8,128]{2,1,0:T(8,128)S(1)}, bf16[128,4096]{1,0:T(8,128)(2,1)S(1)}, bf16[256,512]{1,0:T(8,128)(2,1)S(1)}) custom-call(s32[32]{0:T(128)} %docs_hbm.1, bf16[128,4096]{1,0:T(8,128)(2,1)} %q_hbm.1, bf16[128,512]{1,0:T(8,128)(2,1)} %k_hbm.1, bf16[128,512]{1,0:T(8,128)(2,1)} %v_hbm.1), custom_call_target="tpu_custom_call" | custom-call | tf_op jit(solution)/shard_map/own_block/pallas_call | solution.py:347
  6.3 2.0 %collective-permute-start.4 = (bf16[256,512]{1,0:T(8,128)(2,1)S(1)}, bf16[256,512]{1,0:T(8,128)(2,1)S(1)}, u32[]{:S(2)}, u32[]{:S(2)}) collective-permute-start(bf16[256,512]{1,0:T(8,128)(2,1)S(1)} %get-tuple-element.30.kv_ref), channel_id=1, source_target_pairs={{0,1},{1,4},{2,3},{3,6},{4,2},{5,8},{6,7},{7,10},{8,0},{9,12},{10,... | collective-permute-start | bytes 786440 | tf_op jit(solution)/shard_map/ppermute | solution.py:360
  8.3 1.2 %collective-permute-done.a_ref.ak_ref = bf16[128,512]{1,0:T(8,128)(2,1)S(1)} collective-permute-done((bf16[128,512]{1,0:T(8,128)(2,1)}, bf16[128,512]{1,0:T(8,128)(2,1)S(1)}, u32[]{:S(2)}, u32[]{:S(2)}) %collective-permute-start) | collective-permute-done | bytes 131104 | tf_op jit(solution)/shard_map/ppermute | solution.py:360
  9.5 2.0 %collective-permute-start.5 = (bf16[128,512]{1,0:T(8,128)(2,1)S(1)}, bf16[128,512]{1,0:T(8,128)(2,1)S(1)}, u32[]{:S(2)}, u32[]{:S(2)}) collective-permute-start(bf16[128,512]{1,0:T(8,128)(2,1)S(1)} %collective-permute-done.a_ref.ak_ref), channel_id=1, source_target_pairs={{0,1},{1,0},{2,3},{3,2},{4,5},{5,4},{6,7},{7,6},{8,9},{9,8},{10,11... | collective-permute-start | bytes 393224 | tf_op jit(solution)/shard_map/ppermute | solution.py:360
  11.5 0.0 collective-permute-done.2.beside_v.vs_ref.sv_ref
  11.5 0.0 collective-permute-done.1.beside_k.sk_ref
  11.5 1.3 %early_rows.1 = (bf16[4,1024,128]{2,1,0:T(8,128)(2,1)S(1)}, bf16[4,1024,128]{2,1,0:T(8,128)(2,1)S(1)}, bf16[128,4096]{1,0:T(8,128)(2,1)S(1)}, f32[2,8,128]{2,1,0:T(8,128)S(1)}) custom-call(bf16[128,4096]{1,0:T(8,128)(2,1)S(1)} %get-tuple-element.22.q_ref, f32[3,8,128]{2,1,0:T(8,128)S(1)} %get-tuple-element.23.pen_ref, ...), custom_call_target="tpu_custom_call" | custom-call | tf_op jit(solution)/shard_map/early_rows/pallas_call | solution.py:347
  12.8 0.0 collective-permute-done.3.va_ref.av_ref
  12.8 0.7 %collective-permute-start.6 = (bf16[128,512]{1,0:T(8,128)(2,1)S(1)}, bf16[128,512]{1,0:T(8,128)(2,1)S(1)}, u32[]{:S(2)}, u32[]{:S(2)}) collective-permute-start(bf16[128,512]{1,0:T(8,128)(2,1)S(1)} %collective-permute-done.3.va_ref.av_ref), channel_id=1, source_target_pairs={{0,1},{1,0},{2,3},{3,2},{4,5},{5,4},{6,7},{7,6},{8,9},{9,8},{10,11... | collective-permute-start | bytes 393224 | tf_op jit(solution)/shard_map/ppermute | solution.py:360
  13.5 0.0 collective-permute-done.5.k_ref.bk_ref
  13.5 1.0 %third_weights.1 = (bf16[4,1024,128]{2,1,0:T(8,128)(2,1)S(1)}, bf16[128,4096]{1,0:T(8,128)(2,1)}) custom-call(bf16[128,4096]{1,0:T(8,128)(2,1)S(1)} %get-tuple-element.22.q_ref, f32[3,8,128]{2,1,0:T(8,128)S(1)} %get-tuple-element.23.pen_ref, bf16[128,512]{1,0:T(8,128)(2,1)S(1)} %collective-permute-done.5.k_ref.bk_ref, ...), custom_call_target="tpu_custom_call" | custom-call | tf_op jit(solution)/shard_map/third_weights/pallas_call | solution.py:347
  14.5 0.0 collective-permute-done.6.bv_ref
  14.5 0.1 odd_rows.1
  14.6 0.0 collective-permute-done.4.c_ref
  14.6 17.7 %last_blocks.1 = bf16[128,4096]{1,0:T(8,128)(2,1)} custom-call(bf16[128,4096]{1,0:T(8,128)(2,1)S(1)} %get-tuple-element.22.q_ref, f32[3,8,128]{2,1,0:T(8,128)S(1)} %get-tuple-element.23.pen_ref, f32[4,1024,256]{2,1,0:T(8,128)S(1)} %get-tuple-element.29.both_ref, bf16[256,512]{1,0:T(8,128)(2,1)S(1)} %collective-permute-done.4.c_ref, ...), custom_call_target="tpu_custom_call", output_to_operand_aliasing={{}: (16, {})} | custom-call | tf_op jit(solution)/shard_map/last_blocks/pallas_call | solution.py:347
  (1 shorter events, 0.0 us)
Async XLA Ops:
  0.0 9.5 %collective-permute-start = (bf16[128,512]{1,0:T(8,128)(2,1)}, bf16[128,512]{1,0:T(8,128)(2,1)S(1)}, u32[]{:S(2)}, u32[]{:S(2)}) collective-permute-start(bf16[128,512]{1,0:T(8,128)(2,1)} %k_hbm.1), channel_id=1, source_target_pairs={{0,2},{1,3},{2,4},{3,5},{4,6},{5,7},{6,8},{7,9},{8,10},{9,11},{10,... | collective-permute-start | bytes 393224 | tf_op jit(solution)/shard_map/ppermute | solution.py:360
  2.0 9.4 %collective-permute-start.2 = (bf16[128,512]{1,0:T(8,128)(2,1)}, bf16[128,512]{1,0:T(8,128)(2,1)S(1)}, u32[]{:S(2)}, u32[]{:S(2)}) collective-permute-start(bf16[128,512]{1,0:T(8,128)(2,1)} %v_hbm.1), channel_id=1, source_target_pairs={{0,1},{1,0},{2,3},{3,2},{4,5},{5,4},{6,7},{7,6},{8,9},{9,8},{10,11... | collective-permute-start | bytes 393224 | tf_op jit(solution)/shard_map/ppermute | solution.py:360
  3.0 8.5 %collective-permute-start.1 = (bf16[128,512]{1,0:T(8,128)(2,1)}, bf16[128,512]{1,0:T(8,128)(2,1)S(1)}, u32[]{:S(2)}, u32[]{:S(2)}) collective-permute-start(bf16[128,512]{1,0:T(8,128)(2,1)} %k_hbm.1), channel_id=1, source_target_pairs={{0,1},{1,0},{2,3},{3,2},{4,5},{5,4},{6,7},{7,6},{8,9},{9,8},{10,11... | collective-permute-start | bytes 393224 | tf_op jit(solution)/shard_map/ppermute | solution.py:360
  3.0 9.8 %collective-permute-start.3 = (bf16[128,512]{1,0:T(8,128)(2,1)}, bf16[128,512]{1,0:T(8,128)(2,1)S(1)}, u32[]{:S(2)}, u32[]{:S(2)}) collective-permute-start(bf16[128,512]{1,0:T(8,128)(2,1)} %v_hbm.1), channel_id=1, source_target_pairs={{0,2},{1,3},{2,4},{3,5},{4,6},{5,7},{6,8},{7,9},{8,10},{9,11},{10,... | collective-permute-start | bytes 393224 | tf_op jit(solution)/shard_map/ppermute | solution.py:360
  6.3 8.3 %collective-permute-start.4 = (bf16[256,512]{1,0:T(8,128)(2,1)S(1)}, bf16[256,512]{1,0:T(8,128)(2,1)S(1)}, u32[]{:S(2)}, u32[]{:S(2)}) collective-permute-start(bf16[256,512]{1,0:T(8,128)(2,1)S(1)} %get-tuple-element.30.kv_ref), channel_id=1, source_target_pairs={{0,1},{1,4},{2,3},{3,6},{4,2},{5,8},{6,7},{7,10},{8,0},{9,12},{10,... | collective-permute-start | bytes 786440 | tf_op jit(solution)/shard_map/ppermute | solution.py:360
  9.5 4.0 %collective-permute-start.5 = (bf16[128,512]{1,0:T(8,128)(2,1)S(1)}, bf16[128,512]{1,0:T(8,128)(2,1)S(1)}, u32[]{:S(2)}, u32[]{:S(2)}) collective-permute-start(bf16[128,512]{1,0:T(8,128)(2,1)S(1)} %collective-permute-done.a_ref.ak_ref), channel_id=1, source_target_pairs={{0,1},{1,0},{2,3},{3,2},{4,5},{5,4},{6,7},{7,6},{8,9},{9,8},{10,11... | collective-permute-start | bytes 393224 | tf_op jit(solution)/shard_map/ppermute | solution.py:360
  12.8 1.7 %collective-permute-start.6 = (bf16[128,512]{1,0:T(8,128)(2,1)S(1)}, bf16[128,512]{1,0:T(8,128)(2,1)S(1)}, u32[]{:S(2)}, u32[]{:S(2)}) collective-permute-start(bf16[128,512]{1,0:T(8,128)(2,1)S(1)} %collective-permute-done.3.va_ref.av_ref), channel_id=1, source_target_pairs={{0,1},{1,0},{2,3},{3,2},{4,5},{5,4},{6,7},{7,6},{8,9},{9,8},{10,11... | collective-permute-start | bytes 393224 | tf_op jit(solution)/shard_map/ppermute | solution.py:360

commit v2 on v1

--- a/solution.py
+++ b/solution.py
@@ -107,7 +107,7 @@
         weights_ref[unit[0], unit_rows(unit)] = weigh(scores, pen)
 
 
-def weights_kernel(groups, size, distances, q_ref, pen_ref, k_ref, rows_ref, weights_ref, out_hbm, sem):
+def weights_kernel(groups, size, distances, q_ref, pen_ref, k_ref, kv_ref, sk_ref, sv_ref, so_far, rows_ref, _, weights_ref, out_hbm, result_ref, sem):
     position = lax.axis_index("ctx")
     even, odd = (pen_ref[d - 1][:1] for d in distances)
 
@@ -115,11 +115,19 @@
     def _():
         weigh_all(groups, size, q_ref, jnp.where(lax.rem(position, 2) == 1, odd, even), k_ref, weights_ref)
 
-    @pl.when(position <= 1)
+    @pl.when(position == 1)
     def _():
         copy = pltpu.make_async_copy(rows_ref, out_hbm, sem)
         copy.start()
         copy.wait()
+
+    @pl.when((position <= 1) & jnp.logical_not(is_safe(so_far)))
+    def _():
+        def blocks(g):
+            yield kv_ref[:BLK, cut(g)], kv_ref[BLK:, cut(g)]
+            yield sk_ref[:, cut(g)], sv_ref[:, cut(g)]
+
+        exact_rows(groups, size, q_ref, blocks, [causal_pen(), pen_ref[0][:1]], result_ref, out_hbm, sem)
 
 
 def add_values(unit, weights, values):
@@ -154,8 +162,34 @@
     range_ref[1] = jnp.full((8, HD), jnp.max(low_high[1]), F32)
 
 
+def is_safe(range_ref):
+    in_range = (range_ref[0] > LOW) & (range_ref[1] < HIGH)
+    return jnp.min(jnp.where(in_range, 1.0, 0.0)) > 0.5
+
+
+def exact_rows(groups, size, q_ref, blocks, pens, result_ref, out_hbm, sem):
+    for g in range(groups):
+        keys, values = zip(*blocks(g))
+
+        def one_head(h, _):
+            at = pl.ds(pl.multiple_of((g * size + h) * HD, HD), HD)
+            queries = q_ref[:, at]
+            scores = [dot_nt(queries, x) - pen for x, pen in zip(keys, pens)]
+            top = functools.reduce(jnp.maximum, [jnp.max(x, axis=1, keepdims=True) for x in scores])
+            weights = [jnp.exp2((x - top) * EXP2_SCALE) for x in scores]
+            total = sum(jnp.sum(w, axis=1, keepdims=True) for w in weights)
+            product = sum(dot_nn(w.astype(BF16), x) for w, x in zip(weights, values))
+            result_ref[:, at] = (product / total).astype(BF16)
+            return 0
+
+        lax.fori_loop(0, size, one_head, 0)
+    store = pltpu.make_async_copy(result_ref, out_hbm, sem)
+    store.start()
+    store.wait()
+
+
 def early_kernel(
-    groups, size, q_ref, pen_ref, own_ref, kv_ref, a_ref, beside_k, beside_v, wa_ref, weights_ref, result_ref, range_ref,
+    groups, size, q_ref, pen_ref, own_ref, kv_ref, a_ref, beside_k, beside_v, wa_ref, weights_ref, result_ref, out_hbm, range_ref, sem,
 ):
     position = lax.axis_index("ctx")
     range_ref[...] = jnp.ones_like(range_ref)
@@ -177,20 +211,24 @@
     @pl.when(position == 0)
     def _():
         store_all([own_ref], [part(kv_ref, BLK)])
+        copy = pltpu.make_async_copy(result_ref, out_hbm, sem)
+        copy.start()
+        copy.wait()
 
     @pl.when(position == 1)
     def _():
         store_all([own_ref, weights_ref], [part(kv_ref, BLK), part(beside_v)])
 
 
-def values_kernel(
-    groups, size, own_ref, wa_ref, ws_ref, kv_ref, va_ref, vs_ref, early_range, both_ref, range_ref,
-):
+def values_kernel(groups, size, parity, own_ref, wa_ref, ws_ref, kv_ref, va_ref, vs_ref, so_far, *refs):
+    both_ref, range_ref = refs[-2:]
     position = lax.axis_index("ctx")
-    odd = lax.rem(position, 2) == 1
-    range_ref[...] = early_range[...]
-
-    def whole(weights, values):
+    range_ref[...] = so_far[...]
+
+    @pl.when((lax.rem(position, 2) == parity) & (position > 1))
+    def _():
+        weights = [own_ref, wa_ref] + [ws_ref] * parity
+        values = [part(kv_ref, BLK), part(va_ref)] + [part(vs_ref)] * parity
         low = jnp.ones((BLK, HD), F32)
         for unit in units_of(groups, size, ADD_UNIT):
             both = add_values(unit, weights, values)
@@ -199,17 +237,6 @@
                 low = jnp.minimum(low, both[cut(h, BLK), HD:])
         range_ref[0] = jnp.full((8, HD), jnp.min(low), F32)
 
-    weights = [own_ref, wa_ref]
-    values = [part(kv_ref, BLK), part(va_ref)]
-
-    @pl.when(jnp.logical_not(odd) & (position > 1))
-    def _():
-        whole(weights, values)
-
-    @pl.when(odd & (position > 1))
-    def _():
-        whole(weights + [ws_ref], values + [part(vs_ref)])
-
 
 def out_copies(units, size, result_ref, out_hbm, sems):
     copies = {}
@@ -220,11 +247,15 @@
     return copies
 
 
-def odd_kernel(groups, size, both_ref, wb_ref, bv_ref, so_far, _, out_hbm, range_ref, result_ref, sems):
+def all_here(position):
+    return (lax.rem(position, 2) == 1) | (position < 3)
+
+
+def complete_kernel(groups, size, both_ref, wb_ref, bv_ref, so_far, _, out_hbm, range_ref, result_ref, sems):
     position = lax.axis_index("ctx")
     range_ref[...] = so_far[...]
 
-    @pl.when((lax.rem(position, 2) == 1) & (position > 1))
+    @pl.when(all_here(position) & (position > 1))
     def _():
         units = units_of(groups, size, LAST_UNIT)
         copies = out_copies(units, size, result_ref, out_hbm, sems)
@@ -240,14 +271,22 @@
 
 def last_kernel(
     groups, size, q_ref, pen_ref, both_ref, c_ref, own_ref, wa_ref, wb_ref, ws_ref, kv_ref,
-    ak_ref, av_ref, bk_ref, bv_ref, sk_ref, sv_ref, so_far, _, out_hbm, result_ref, range_ref, sems,
+    ak_ref, av_ref, bk_ref, bv_ref, sk_ref, sv_ref, so_far, _, out_hbm, result_ref, range_ref, safe_ref, sems,
 ):
     position = lax.axis_index("ctx")
     odd = lax.rem(position, 2) == 1
     units = units_of(groups, size, LAST_UNIT)
     copies = out_copies(units, size, result_ref, out_hbm, sems)
     range_ref[...] = so_far[...]
-    waits = jnp.logical_not(odd) & (position > 1)
+    waits = jnp.logical_not(all_here(position))
+    safe_ref[0] = 1
+
+    def check():
+        safe_ref[0] = jnp.where(is_safe(range_ref), 1, 0)
+
+    @pl.when(jnp.logical_not(waits) & (position > 1))
+    def _():
+        check()
 
     @pl.when(waits)
     def _():
@@ -267,40 +306,22 @@
 
         staggered(units, first, second)
         note_range(low_high, range_ref)
-
-    safe = (jnp.min(range_ref[0]) > LOW) & (jnp.max(range_ref[1]) < HIGH)
-
-    @pl.when(waits)
-    def _():
+        check()
         for copy in copies.values():
             copy.wait()
 
-    @pl.when(jnp.logical_not(safe))
+    @pl.when(safe_ref[0] == 0)
     def _():
         pens = [causal_pen()] + [pen_ref[i][:1] for i in range(3)]
         pairs = (((bk_ref, bv_ref, 0), (sk_ref, sv_ref, 0)), ((ak_ref, av_ref, 0),) * 2, ((c_ref, c_ref, BLK), (bk_ref, bv_ref, 0)))
-        for g in range(groups):
-            keys = [kv_ref[:BLK, cut(g)]]
-            values = [kv_ref[BLK:, cut(g)]]
+
+        def blocks(g):
+            yield kv_ref[:BLK, cut(g)], kv_ref[BLK:, cut(g)]
             for (ek, ev, first), (ok, ov, _) in pairs:
-                keys.append(jnp.where(odd, ok[:BLK, cut(g)], ek[:BLK, cut(g)]))
-                values.append(jnp.where(odd, ov[:BLK, cut(g)], ev[first : first + BLK, cut(g)]))
-
-            def one_head(h, _):
-                at = pl.ds(pl.multiple_of((g * size + h) * HD, HD), HD)
-                queries = q_ref[:, at]
-                scores = [dot_nt(queries, x) - pen for x, pen in zip(keys, pens)]
-                top = functools.reduce(jnp.maximum, [jnp.max(x, axis=1, keepdims=True) for x in scores])
-                weights = [jnp.exp2((x - top) * EXP2_SCALE) for x in scores]
-                total = sum(jnp.sum(w, axis=1, keepdims=True) for w in weights)
-                product = sum(dot_nn(w.astype(BF16), x) for w, x in zip(weights, values))
-                result_ref[:, at] = (product / total).astype(BF16)
-                return 0
-
-            lax.fori_loop(0, size, one_head, 0)
-        store = pltpu.make_async_copy(result_ref, out_hbm, sems.at[0])
-        store.start()
-        store.wait()
+                key = jnp.where(odd, ok[:BLK, cut(g)], ek[:BLK, cut(g)])
+                yield key, jnp.where(odd, ov[:BLK, cut(g)], ev[first : first + BLK, cut(g)])
+
+        exact_rows(groups, size, q_ref, blocks, pens, result_ref, out_hbm, sems.at[0])
 
 
 def routes(n):
@@ -326,7 +347,7 @@
     return lax.optimization_barrier((value, *others))[0]
 
 
-def on_device(queries, keys, values, docs):
+def on_device(queries, keys, values_in, docs):
     row_count, width = keys.shape
     groups = width // HD
     size = queries.shape[1] // width
@@ -363,37 +384,45 @@
         return call(
             functools.partial(own_kernel, groups, size), "own_block",
             (weights_shape, jax.ShapeDtypeStruct((3, 8, HD), F32), result, pack_shape),
-            [in_hbm(x) for x in (docs, queries, keys, values)], in_specs=[HBM] * 4,
+            [in_hbm(x) for x in (docs, queries, keys, values_in)], in_specs=[HBM] * 4,
             scratch_shapes=[pltpu.SMEM(docs.shape, jnp.int32), dma((groups + 3,))],
         )
 
     def early(*operands):
         return call(
             functools.partial(early_kernel, groups, size), "early_rows",
-            (weights_shape, weights_shape, result, range_shape), operands,
+            (weights_shape, weights_shape, result, result, range_shape), operands,
+            out_specs=(VMEM, VMEM, VMEM, HBM, VMEM), scratch_shapes=[dma(())],
+        )
+
+    def values(parity, *operands):
+        name = ("even", "odd")[parity] + "_values"
+        alias = {7: 0} if len(operands) > 7 else {}
+        return call(
+            functools.partial(values_kernel, groups, size, parity), name, (both_shape, range_shape), operands,
+            input_output_aliases=alias,
         )
 
     def weigh_block(name, distances, *operands):
         return call(
             functools.partial(weights_kernel, groups, size, distances), name, (weights_shape, result), operands,
-            out_specs=(VMEM, HBM), scratch_shapes=[dma(())],
+            in_specs=[VMEM] * 8 + [HBM], out_specs=(VMEM, HBM), input_output_aliases={8: 1},
+            scratch_shapes=[pltpu.VMEM(result.shape, BF16), dma(())],
         )
 
-    ak, av = move(keys, ring), move(values, ring)
-    sk, sv = move(keys, swap), move(values, swap)
+    ak, av = move(keys, ring), move(values_in, ring)
+    sk, sv = move(keys, swap), move(values_in, swap)
     w_own, pen, local, block = own()
     block_c = move(after(block, pen), across)
-    w_a, w_s, first_rows, early_range = early(local, pen, w_own, block, ak, sk, sv)
+    w_a, w_s, first_rows, stored, early_range = early(local, pen, w_own, block, ak, sk, sv)
     bk = move(after(ak, pen), swap)
-    bv = move(after(av, w_a), swap)
-    w_b, stored = weigh_block("third_weights", (1, 3), local, pen, bk, first_rows)
-    both, early_range = call(
-        functools.partial(values_kernel, groups, size), "values", (both_shape, range_shape),
-        (w_own, w_a, w_s, block, av, sv, early_range),
-    )
+    both, so_far = values(1, w_own, w_a, w_s, block, av, sv, early_range)
+    bv = move(after(av, both), swap)
+    both, so_far = values(0, w_own, w_a, w_s, block, av, sv, so_far, both)
+    w_b, stored = weigh_block("third_weights", (1, 3), local, pen, bk, block, sk, sv, early_range, first_rows, in_hbm(stored))
     unit_sems = dma((groups * size // LAST_UNIT,))
     stored, so_far = call(
-        functools.partial(odd_kernel, groups, size), "odd_rows", (result, range_shape), (both, w_b, bv, early_range, in_hbm(stored)),
+        functools.partial(complete_kernel, groups, size), "complete_rows", (result, range_shape), (both, w_b, bv, so_far, in_hbm(stored)),
         in_specs=[VMEM] * 4 + [HBM], out_specs=(HBM, VMEM), input_output_aliases={4: 0},
         scratch_shapes=[pltpu.VMEM(result.shape, BF16), unit_sems],
     )
@@ -401,7 +430,7 @@
     return call(
         functools.partial(last_kernel, groups, size), "last_blocks", result, operands,
         in_specs=[VMEM] * 16 + [HBM], out_specs=HBM, input_output_aliases={16: 0},
-        scratch_shapes=[pltpu.VMEM(result.shape, BF16), pltpu.VMEM(range_shape.shape, F32), unit_sems],
+        scratch_shapes=[pltpu.VMEM(result.shape, BF16), pltpu.VMEM(range_shape.shape, F32), pltpu.SMEM((1,), jnp.int32), unit_sems],
     )
 
 

time: 32.7 us -> 32 us (0.979)
  the two profiles are of different devices: /device:TPU:1 before, /device:TPU:25 now
where the time goes in v2:
time: 32 us; the launch traced here: 31.8 us
  Pallas kernels  24.3 us (76%)
  starting transfers between devices  6.22 us (19%)
  waiting for transfers between devices  1.29 us (4%)
    pallas_call x7, Pallas kernels, call(): pl.pallas_call(kernel, out_shape=out_shape, in_specs=in_specs or [VMEM] *...  24.3 us
    ppermute x7, starting transfers between devices, move(): return lax.ppermute(block, 'ctx', route)  6.22 us
    ppermute x7, waiting for transfers between devices, move(): return lax.ppermute(block, 'ctx', route)  1.29 us
  transfers between devices with their start and end apart: 7, of which 3 were waited for; matrix products, arithmetic and copies ran while one was open for 0% of the time, Pallas kernels for 21%

profile of v2, /device:TPU:25, one launch (start us, length us, event | category | flops | bytes accessed | tf_op | source)
XLA Modules:
  0.0 31.8 jit_solution(13049929395909532228)
XLA Ops:
  0.0 1.2 %collective-permute-start = (bf16[128,512]{1,0:T(8,128)(2,1)}, bf16[128,512]{1,0:T(8,128)(2,1)S(1)}, u32[]{:S(2)}, u32[]{:S(2)}) collective-permute-start(bf16[128,512]{1,0:T(8,128)(2,1)} %k_hbm.1), channel_id=1, source_target_pairs={{0,2},{1,3},{2,4},{3,5},{4,6},{5,7},{6,8},{7,9},{8,10},{9,11},{10,... | collective-permute-start | bytes 393224 | tf_op jit(solution)/shard_map/ppermute | solution.py:381
  1.2 1.0 %collective-permute-start.1 = (bf16[128,512]{1,0:T(8,128)(2,1)}, bf16[128,512]{1,0:T(8,128)(2,1)S(1)}, u32[]{:S(2)}, u32[]{:S(2)}) collective-permute-start(bf16[128,512]{1,0:T(8,128)(2,1)} %k_hbm.1), channel_id=1, source_target_pairs={{0,1},{1,0},{2,3},{3,2},{4,5},{5,4},{6,7},{7,6},{8,9},{9,8},{10,11... | collective-permute-start | bytes 393224 | tf_op jit(solution)/shard_map/ppermute | solution.py:381
  2.2 0.0 collective-permute-start.2
  2.2 1.2 %collective-permute-start.3 = (bf16[128,512]{1,0:T(8,128)(2,1)}, bf16[128,512]{1,0:T(8,128)(2,1)S(1)}, u32[]{:S(2)}, u32[]{:S(2)}) collective-permute-start(bf16[128,512]{1,0:T(8,128)(2,1)} %v_hbm.1), channel_id=1, source_target_pairs={{0,2},{1,3},{2,4},{3,5},{4,6},{5,7},{6,8},{7,9},{8,10},{9,11},{10,... | collective-permute-start | bytes 393224 | tf_op jit(solution)/shard_map/ppermute | solution.py:381
  3.4 2.1 %own_block.1 = (bf16[4,1024,128]{2,1,0:T(8,128)(2,1)S(1)}, f32[3,8,128]{2,1,0:T(8,128)S(1)}, bf16[128,4096]{1,0:T(8,128)(2,1)S(1)}, bf16[256,512]{1,0:T(8,128)(2,1)S(1)}) custom-call(s32[32]{0:T(128)} %docs_hbm.1, bf16[128,4096]{1,0:T(8,128)(2,1)} %q_hbm.1, bf16[128,512]{1,0:T(8,128)(2,1)} %k_hbm.1, bf16[128,512]{1,0:T(8,128)(2,1)} %v_hbm.1), custom_call_target="tpu_custom_call" | custom-call | tf_op jit(solution)/shard_map/own_block/pallas_call | solution.py:368
  5.5 0.5 %collective-permute-start.4 = (bf16[256,512]{1,0:T(8,128)(2,1)S(1)}, bf16[256,512]{1,0:T(8,128)(2,1)S(1)}, u32[]{:S(2)}, u32[]{:S(2)}) collective-permute-start(bf16[256,512]{1,0:T(8,128)(2,1)S(1)} %get-tuple-element.35.kv_ref), channel_id=1, source_target_pairs={{0,1},{1,4},{2,3},{3,6},{4,2},{5,8},{6,7},{7,10},{8,0},{9,12},{10,... | collective-permute-start | bytes 786440 | tf_op jit(solution)/shard_map/ppermute | solution.py:381
  6.0 0.4 %collective-permute-done.a_ref.ak_ref = bf16[128,512]{1,0:T(8,128)(2,1)S(1)} collective-permute-done((bf16[128,512]{1,0:T(8,128)(2,1)}, bf16[128,512]{1,0:T(8,128)(2,1)S(1)}, u32[]{:S(2)}, u32[]{:S(2)}) %collective-permute-start) | collective-permute-done | bytes 131104 | tf_op jit(solution)/shard_map/ppermute | solution.py:381
  6.4 2.2 %collective-permute-start.5 = (bf16[128,512]{1,0:T(8,128)(2,1)S(1)}, bf16[128,512]{1,0:T(8,128)(2,1)S(1)}, u32[]{:S(2)}, u32[]{:S(2)}) collective-permute-start(bf16[128,512]{1,0:T(8,128)(2,1)S(1)} %collective-permute-done.a_ref.ak_ref), channel_id=1, source_target_pairs={{0,1},{1,0},{2,3},{3,2},{4,5},{5,4},{6,7},{7,6},{8,9},{9,8},{10,11... | collective-permute-start | bytes 393224 | tf_op jit(solution)/shard_map/ppermute | solution.py:381
  8.6 0.0 collective-permute-done.1.beside_k.sk_ref
  8.6 0.0 collective-permute-done.2.beside_v.vs_ref.sv_ref
  8.6 0.9 %early_rows.1 = (bf16[4,1024,128]{2,1,0:T(8,128)(2,1)S(1)}, bf16[4,1024,128]{2,1,0:T(8,128)(2,1)S(1)}, bf16[128,4096]{1,0:T(8,128)(2,1)S(1)}, bf16[128,4096]{1,0:T(8,128)(2,1)}, f32[2,8,128]{2,1,0:T(8,128)S(1)}) custom-call(bf16[128,4096]{1,0:T(8,128)(2,1)S(1)} %get-tuple-element.25.q_ref, f32[3,8,128]{2,1,0:T(8,128)S(1)} %get-tuple-element.26.pen_ref, ...), custom_call_target="tpu_custom_call" | custom-call | tf_op jit(solution)/shard_map/early_rows/pallas_call | solution.py:368
  9.5 0.2 collective-permute-done.3.va_ref.av_ref
  9.7 1.4 %odd_values.1 = (f32[4,1024,256]{2,1,0:T(8,128)S(1)}, f32[2,8,128]{2,1,0:T(8,128)S(1)}) custom-call(bf16[4,1024,128]{2,1,0:T(8,128)(2,1)S(1)} %get-tuple-element.27.own_ref, bf16[4,1024,128]{2,1,0:T(8,128)(2,1)S(1)} %get-tuple-element.29.wa_ref, bf16[4,1024,128]{2,1,0:T(8,128)(2,1)S(1)} %get-tuple-element.30.ws_ref, ...), custom_call_target="tpu_custom_call" | custom-call | tf_op jit(solution)/shard_map/odd_values/pallas_call | solution.py:368
  11.1 0.2 collective-permute-start.6
  11.3 0.0 collective-permute-done.5.k_ref.bk_ref
  11.3 0.6 %third_weights.1 = (bf16[4,1024,128]{2,1,0:T(8,128)(2,1)S(1)}, bf16[128,4096]{1,0:T(8,128)(2,1)}) custom-call(bf16[128,4096]{1,0:T(8,128)(2,1)S(1)} %get-tuple-element.25.q_ref, f32[3,8,128]{2,1,0:T(8,128)S(1)} %get-tuple-element.26.pen_ref, bf16[128,512]{1,0:T(8,128)(2,1)S(1)} %collective-permute-done.5.k_ref.bk_ref, ...), custom_call_target="tpu_custom_call", output_to_operand_aliasing={{1}: (8, {})} | custom-call | tf_op jit(solution)/shard_map/third_weights/pallas_call | solution.py:368
  11.8 0.6 %collective-permute-done.6.bv_ref = bf16[128,512]{1,0:T(8,128)(2,1)S(1)} collective-permute-done((bf16[128,512]{1,0:T(8,128)(2,1)S(1)}, bf16[128,512]{1,0:T(8,128)(2,1)S(1)}, u32[]{:S(2)}, u32[]{:S(2)}) %collective-permute-start.6) | collective-permute-done | bytes 131104 | tf_op jit(solution)/shard_map/ppermute | solution.py:381
  12.5 1.6 %complete_rows.1 = (bf16[128,4096]{1,0:T(8,128)(2,1)}, f32[2,8,128]{2,1,0:T(8,128)S(1)}) custom-call(f32[4,1024,256]{2,1,0:T(8,128)S(1)} %get-tuple-element.34.both_ref, bf16[4,1024,128]{2,1,0:T(8,128)(2,1)S(1)} %get-tuple-element.39.wb_ref, bf16[128,512]{1,0:T(8,128)(2,1)S(1)} %collective-permute-done.6.bv_ref, ...), custom_call_target="tpu_custom_call", output_to_operand_aliasing={{0}: (4, {})} | custom-call | tf_op jit(solution)/shard_map/complete_rows/pallas_call | solution.py:368
  14.1 0.0 collective-permute-done.4.c_ref
  14.1 17.7 %last_blocks.1 = bf16[128,4096]{1,0:T(8,128)(2,1)} custom-call(bf16[128,4096]{1,0:T(8,128)(2,1)S(1)} %get-tuple-element.25.q_ref, f32[3,8,128]{2,1,0:T(8,128)S(1)} %get-tuple-element.26.pen_ref, f32[4,1024,256]{2,1,0:T(8,128)S(1)} %get-tuple-element.34.both_ref, bf16[256,512]{1,0:T(8,128)(2,1)S(1)} %collective-permute-done.4.c_ref, ...), custom_call_target="tpu_custom_call", output_to_operand_aliasing={{}: (16, {})} | custom-call | tf_op jit(solution)/shard_map/last_blocks/pallas_call | solution.py:368
  (1 shorter events, 0.0 us)
Async XLA Ops:
  0.0 6.4 %collective-permute-start = (bf16[128,512]{1,0:T(8,128)(2,1)}, bf16[128,512]{1,0:T(8,128)(2,1)S(1)}, u32[]{:S(2)}, u32[]{:S(2)}) collective-permute-start(bf16[128,512]{1,0:T(8,128)(2,1)} %k_hbm.1), channel_id=1, source_target_pairs={{0,2},{1,3},{2,4},{3,5},{4,6},{5,7},{6,8},{7,9},{8,10},{9,11},{10,... | collective-permute-start | bytes 393224 | tf_op jit(solution)/shard_map/ppermute | solution.py:381
  1.2 7.3 %collective-permute-start.1 = (bf16[128,512]{1,0:T(8,128)(2,1)}, bf16[128,512]{1,0:T(8,128)(2,1)S(1)}, u32[]{:S(2)}, u32[]{:S(2)}) collective-permute-start(bf16[128,512]{1,0:T(8,128)(2,1)} %k_hbm.1), channel_id=1, source_target_pairs={{0,1},{1,0},{2,3},{3,2},{4,5},{5,4},{6,7},{7,6},{8,9},{9,8},{10,11... | collective-permute-start | bytes 393224 | tf_op jit(solution)/shard_map/ppermute | solution.py:381
  2.2 6.4 %collective-permute-start.2 = (bf16[128,512]{1,0:T(8,128)(2,1)}, bf16[128,512]{1,0:T(8,128)(2,1)S(1)}, u32[]{:S(2)}, u32[]{:S(2)}) collective-permute-start(bf16[128,512]{1,0:T(8,128)(2,1)} %v_hbm.1), channel_id=1, source_target_pairs={{0,1},{1,0},{2,3},{3,2},{4,5},{5,4},{6,7},{7,6},{8,9},{9,8},{10,11... | collective-permute-start | bytes 393224 | tf_op jit(solution)/shard_map/ppermute | solution.py:381
  2.2 7.5 %collective-permute-start.3 = (bf16[128,512]{1,0:T(8,128)(2,1)}, bf16[128,512]{1,0:T(8,128)(2,1)S(1)}, u32[]{:S(2)}, u32[]{:S(2)}) collective-permute-start(bf16[128,512]{1,0:T(8,128)(2,1)} %v_hbm.1), channel_id=1, source_target_pairs={{0,2},{1,3},{2,4},{3,5},{4,6},{5,7},{6,8},{7,9},{8,10},{9,11},{10,... | collective-permute-start | bytes 393224 | tf_op jit(solution)/shard_map/ppermute | solution.py:381
  5.5 8.6 %collective-permute-start.4 = (bf16[256,512]{1,0:T(8,128)(2,1)S(1)}, bf16[256,512]{1,0:T(8,128)(2,1)S(1)}, u32[]{:S(2)}, u32[]{:S(2)}) collective-permute-start(bf16[256,512]{1,0:T(8,128)(2,1)S(1)} %get-tuple-element.35.kv_ref), channel_id=1, source_target_pairs={{0,1},{1,4},{2,3},{3,6},{4,2},{5,8},{6,7},{7,10},{8,0},{9,12},{10,... | collective-permute-start | bytes 786440 | tf_op jit(solution)/shard_map/ppermute | solution.py:381
  6.4 4.9 %collective-permute-start.5 = (bf16[128,512]{1,0:T(8,128)(2,1)S(1)}, bf16[128,512]{1,0:T(8,128)(2,1)S(1)}, u32[]{:S(2)}, u32[]{:S(2)}) collective-permute-start(bf16[128,512]{1,0:T(8,128)(2,1)S(1)} %collective-permute-done.a_ref.ak_ref), channel_id=1, source_target_pairs={{0,1},{1,0},{2,3},{3,2},{4,5},{5,4},{6,7},{7,6},{8,9},{9,8},{10,11... | collective-permute-start | bytes 393224 | tf_op jit(solution)/shard_map/ppermute | solution.py:381
  11.1 1.4 %collective-permute-start.6 = (bf16[128,512]{1,0:T(8,128)(2,1)S(1)}, bf16[128,512]{1,0:T(8,128)(2,1)S(1)}, u32[]{:S(2)}, u32[]{:S(2)}) collective-permute-start(bf16[128,512]{1,0:T(8,128)(2,1)S(1)} %collective-permute-done.3.va_ref.av_ref), channel_id=1, source_target_pairs={{0,1},{1,0},{2,3},{3,2},{4,5},{5,4},{6,7},{7,6},{8,9},{9,8},{10,11... | collective-permute-start | bytes 393224 | tf_op jit(solution)/shard_map/ppermute | solution.py:381

commit v3 on v2

--- a/solution.py
+++ b/solution.py
@@ -189,7 +189,7 @@
 
 
 def early_kernel(
-    groups, size, q_ref, pen_ref, own_ref, kv_ref, a_ref, beside_k, beside_v, wa_ref, weights_ref, result_ref, out_hbm, range_ref, sem,
+    groups, size, q_ref, pen_ref, own_ref, kv_ref, a_ref, beside_k, wa_ref, weights_ref, out_hbm, range_ref, result_ref, sem,
 ):
     position = lax.axis_index("ctx")
     range_ref[...] = jnp.ones_like(range_ref)
@@ -215,13 +215,9 @@
         copy.start()
         copy.wait()
 
-    @pl.when(position == 1)
-    def _():
-        store_all([own_ref, weights_ref], [part(kv_ref, BLK), part(beside_v)])
-
 
 def values_kernel(groups, size, parity, own_ref, wa_ref, ws_ref, kv_ref, va_ref, vs_ref, so_far, *refs):
-    both_ref, range_ref = refs[-2:]
+    both_ref, range_ref = refs[-2 - parity : len(refs) - parity]
     position = lax.axis_index("ctx")
     range_ref[...] = so_far[...]
 
@@ -236,6 +232,16 @@
             for h in range(unit[2]):
                 low = jnp.minimum(low, both[cut(h, BLK), HD:])
         range_ref[0] = jnp.full((8, HD), jnp.min(low), F32)
+
+    if parity == 1:
+
+        @pl.when(position == 1)
+        def _():
+            low_high = new_range()
+            for unit in units_of(groups, size, ADD_UNIT):
+                both = add_values(unit, [own_ref, ws_ref], [part(kv_ref, BLK), part(vs_ref)])
+                finish(size, unit, both, refs[-1], low_high)
+            note_range(low_high, range_ref)
 
 
 def out_copies(units, size, result_ref, out_hbm, sems):
@@ -391,15 +397,16 @@
     def early(*operands):
         return call(
             functools.partial(early_kernel, groups, size), "early_rows",
-            (weights_shape, weights_shape, result, result, range_shape), operands,
-            out_specs=(VMEM, VMEM, VMEM, HBM, VMEM), scratch_shapes=[dma(())],
+            (weights_shape, weights_shape, result, range_shape), operands,
+            out_specs=(VMEM, VMEM, HBM, VMEM), scratch_shapes=[pltpu.VMEM(result.shape, BF16), dma(())],
         )
 
     def values(parity, *operands):
         name = ("even", "odd")[parity] + "_values"
         alias = {7: 0} if len(operands) > 7 else {}
         return call(
-            functools.partial(values_kernel, groups, size, parity), name, (both_shape, range_shape), operands,
+            functools.partial(values_kernel, groups, size, parity), name,
+            (both_shape, range_shape) + (result,) * parity, operands,
             input_output_aliases=alias,
         )
 
@@ -414,12 +421,13 @@
     sk, sv = move(keys, swap), move(values_in, swap)
     w_own, pen, local, block = own()
     block_c = move(after(block, pen), across)
-    w_a, w_s, first_rows, stored, early_range = early(local, pen, w_own, block, ak, sk, sv)
+    w_a, w_s, stored, early_range = early(local, pen, w_own, block, ak, sk)
     bk = move(after(ak, pen), swap)
-    both, so_far = values(1, w_own, w_a, w_s, block, av, sv, early_range)
+    both, so_far, first_rows = values(1, w_own, w_a, w_s, block, av, sv, early_range)
+    first_range = so_far
     bv = move(after(av, both), swap)
     both, so_far = values(0, w_own, w_a, w_s, block, av, sv, so_far, both)
-    w_b, stored = weigh_block("third_weights", (1, 3), local, pen, bk, block, sk, sv, early_range, first_rows, in_hbm(stored))
+    w_b, stored = weigh_block("third_weights", (1, 3), local, pen, bk, block, sk, sv, first_range, first_rows, in_hbm(stored))
     unit_sems = dma((groups * size // LAST_UNIT,))
     stored, so_far = call(
         functools.partial(complete_kernel, groups, size), "complete_rows", (result, range_shape), (both, w_b, bv, so_far, in_hbm(stored)),

time: 32 us -> 32 us (level)
  the two profiles are of different devices: /device:TPU:25 before, /device:TPU:17 now
where the time goes in v3:
time: 32 us; the launch traced here: 31.9 us
  Pallas kernels  24.2 us (76%)
  starting transfers between devices  6.94 us (22%)
  waiting for transfers between devices  0.61 us (2%)
    pallas_call x7, Pallas kernels, call(): pl.pallas_call(kernel, out_shape=out_shape, in_specs=in_specs or [VMEM] *...  24.2 us
    ppermute x7, starting transfers between devices, move(): return lax.ppermute(block, 'ctx', route)  6.94 us
  transfers between devices with their start and end apart: 7, of which 2 were waited for; matrix products, arithmetic and copies ran while one was open for 0% of the time, Pallas kernels for 20%

profile of v3, /device:TPU:17, one launch (start us, length us, event | category | flops | bytes accessed | tf_op | source)
XLA Modules:
  0.0 31.9 jit_solution(18260384953163597641)
XLA Ops:
  0.0 1.2 %collective-permute-start = (bf16[128,512]{1,0:T(8,128)(2,1)}, bf16[128,512]{1,0:T(8,128)(2,1)S(1)}, u32[]{:S(2)}, u32[]{:S(2)}) collective-permute-start(bf16[128,512]{1,0:T(8,128)(2,1)} %k_hbm.1), channel_id=1, source_target_pairs={{0,2},{1,3},{2,4},{3,5},{4,6},{5,7},{6,8},{7,9},{8,10},{9,11},{10,... | collective-permute-start | bytes 393224 | tf_op jit(solution)/shard_map/ppermute | solution.py:387
  1.2 1.0 %collective-permute-start.1 = (bf16[128,512]{1,0:T(8,128)(2,1)}, bf16[128,512]{1,0:T(8,128)(2,1)S(1)}, u32[]{:S(2)}, u32[]{:S(2)}) collective-permute-start(bf16[128,512]{1,0:T(8,128)(2,1)} %k_hbm.1), channel_id=1, source_target_pairs={{0,1},{1,0},{2,3},{3,2},{4,5},{5,4},{6,7},{7,6},{8,9},{9,8},{10,11... | collective-permute-start | bytes 393224 | tf_op jit(solution)/shard_map/ppermute | solution.py:387
  2.2 1.2 %collective-permute-start.2 = (bf16[128,512]{1,0:T(8,128)(2,1)}, bf16[128,512]{1,0:T(8,128)(2,1)S(1)}, u32[]{:S(2)}, u32[]{:S(2)}) collective-permute-start(bf16[128,512]{1,0:T(8,128)(2,1)} %v_hbm.1), channel_id=1, source_target_pairs={{0,2},{1,3},{2,4},{3,5},{4,6},{5,7},{6,8},{7,9},{8,10},{9,11},{10,... | collective-permute-start | bytes 393224 | tf_op jit(solution)/shard_map/ppermute | solution.py:387
  3.4 0.3 collective-permute-start.3
  3.7 2.1 %own_block.1 = (bf16[4,1024,128]{2,1,0:T(8,128)(2,1)S(1)}, f32[3,8,128]{2,1,0:T(8,128)S(1)}, bf16[128,4096]{1,0:T(8,128)(2,1)S(1)}, bf16[256,512]{1,0:T(8,128)(2,1)S(1)}) custom-call(s32[32]{0:T(128)} %docs_hbm.1, bf16[128,4096]{1,0:T(8,128)(2,1)} %q_hbm.1, bf16[128,512]{1,0:T(8,128)(2,1)} %k_hbm.1, bf16[128,512]{1,0:T(8,128)(2,1)} %v_hbm.1), custom_call_target="tpu_custom_call" | custom-call | tf_op jit(solution)/shard_map/own_block/pallas_call | solution.py:374
  5.7 1.4 %collective-permute-start.4 = (bf16[256,512]{1,0:T(8,128)(2,1)S(1)}, bf16[256,512]{1,0:T(8,128)(2,1)S(1)}, u32[]{:S(2)}, u32[]{:S(2)}) collective-permute-start(bf16[256,512]{1,0:T(8,128)(2,1)S(1)} %get-tuple-element.35.kv_ref), channel_id=1, source_target_pairs={{0,1},{1,4},{2,3},{3,6},{4,2},{5,8},{6,7},{7,10},{8,0},{9,12},{10,... | collective-permute-start | bytes 786440 | tf_op jit(solution)/shard_map/ppermute | solution.py:387
  7.2 0.0 collective-permute-done.a_ref.ak_ref
  7.2 1.4 %collective-permute-start.5 = (bf16[128,512]{1,0:T(8,128)(2,1)S(1)}, bf16[128,512]{1,0:T(8,128)(2,1)S(1)}, u32[]{:S(2)}, u32[]{:S(2)}) collective-permute-start(bf16[128,512]{1,0:T(8,128)(2,1)S(1)} %collective-permute-done.a_ref.ak_ref), channel_id=1, source_target_pairs={{0,1},{1,0},{2,3},{3,2},{4,5},{5,4},{6,7},{7,6},{8,9},{9,8},{10,11... | collective-permute-start | bytes 393224 | tf_op jit(solution)/shard_map/ppermute | solution.py:387
  8.6 0.0 collective-permute-done.1.beside_k.sk_ref
  8.6 0.9 %early_rows.1 = (bf16[4,1024,128]{2,1,0:T(8,128)(2,1)S(1)}, bf16[4,1024,128]{2,1,0:T(8,128)(2,1)S(1)}, bf16[128,4096]{1,0:T(8,128)(2,1)}, f32[2,8,128]{2,1,0:T(8,128)S(1)}) custom-call(bf16[128,4096]{1,0:T(8,128)(2,1)S(1)} %get-tuple-element.25.q_ref, f32[3,8,128]{2,1,0:T(8,128)S(1)} %get-tuple-element.26.pen_ref, ...), custom_call_target="tpu_custom_call" | custom-call | tf_op jit(solution)/shard_map/early_rows/pallas_call | solution.py:374
  9.5 0.2 collective-permute-done.2.va_ref.av_ref
  9.7 0.0 collective-permute-done.3.vs_ref.sv_ref
  9.7 1.4 %odd_values.1 = (f32[4,1024,256]{2,1,0:T(8,128)S(1)}, f32[2,8,128]{2,1,0:T(8,128)S(1)}, bf16[128,4096]{1,0:T(8,128)(2,1)S(1)}) custom-call(bf16[4,1024,128]{2,1,0:T(8,128)(2,1)S(1)} %get-tuple-element.27.own_ref, bf16[4,1024,128]{2,1,0:T(8,128)(2,1)S(1)} %get-tuple-element.29.wa_ref, bf16[4,1024,128]{2,1,0:T(8,128)(2,1)S(1)} %get-tuple-element.30.ws_ref, ...), custom_call_target="tpu_custom_call" | custom-call | tf_op jit(solution)/shard_map/odd_values/pallas_call | solution.py:374
  11.1 0.5 %collective-permute-start.6 = (bf16[128,512]{1,0:T(8,128)(2,1)S(1)}, bf16[128,512]{1,0:T(8,128)(2,1)S(1)}, u32[]{:S(2)}, u32[]{:S(2)}) collective-permute-start(bf16[128,512]{1,0:T(8,128)(2,1)S(1)} %collective-permute-done.2.va_ref.av_ref), channel_id=1, source_target_pairs={{0,1},{1,0},{2,3},{3,2},{4,5},{5,4},{6,7},{7,6},{8,9},{9,8},{10,11... | collective-permute-start | bytes 393224 | tf_op jit(solution)/shard_map/ppermute | solution.py:387
  11.6 0.0 collective-permute-done.5.k_ref.bk_ref
  11.6 0.6 %third_weights.1 = (bf16[4,1024,128]{2,1,0:T(8,128)(2,1)S(1)}, bf16[128,4096]{1,0:T(8,128)(2,1)}) custom-call(bf16[128,4096]{1,0:T(8,128)(2,1)S(1)} %get-tuple-element.25.q_ref, f32[3,8,128]{2,1,0:T(8,128)S(1)} %get-tuple-element.26.pen_ref, bf16[128,512]{1,0:T(8,128)(2,1)S(1)} %collective-permute-done.5.k_ref.bk_ref, ...), custom_call_target="tpu_custom_call", output_to_operand_aliasing={{1}: (8, {})} | custom-call | tf_op jit(solution)/shard_map/third_weights/pallas_call | solution.py:374
  12.1 0.4 %collective-permute-done.6.bv_ref = bf16[128,512]{1,0:T(8,128)(2,1)S(1)} collective-permute-done((bf16[128,512]{1,0:T(8,128)(2,1)S(1)}, bf16[128,512]{1,0:T(8,128)(2,1)S(1)}, u32[]{:S(2)}, u32[]{:S(2)}) %collective-permute-start.6) | collective-permute-done | bytes 131104 | tf_op jit(solution)/shard_map/ppermute | solution.py:387
  12.5 1.6 %complete_rows.1 = (bf16[128,4096]{1,0:T(8,128)(2,1)}, f32[2,8,128]{2,1,0:T(8,128)S(1)}) custom-call(f32[4,1024,256]{2,1,0:T(8,128)S(1)} %get-tuple-element.34.both_ref, bf16[4,1024,128]{2,1,0:T(8,128)(2,1)S(1)} %get-tuple-element.39.wb_ref, bf16[128,512]{1,0:T(8,128)(2,1)S(1)} %collective-permute-done.6.bv_ref, ...), custom_call_target="tpu_custom_call", output_to_operand_aliasing={{0}: (4, {})} | custom-call | tf_op jit(solution)/shard_map/complete_rows/pallas_call | solution.py:374
  14.1 0.0 collective-permute-done.4.c_ref
  14.1 17.7 %last_blocks.1 = bf16[128,4096]{1,0:T(8,128)(2,1)} custom-call(bf16[128,4096]{1,0:T(8,128)(2,1)S(1)} %get-tuple-element.25.q_ref, f32[3,8,128]{2,1,0:T(8,128)S(1)} %get-tuple-element.26.pen_ref, f32[4,1024,256]{2,1,0:T(8,128)S(1)} %get-tuple-element.34.both_ref, bf16[256,512]{1,0:T(8,128)(2,1)S(1)} %collective-permute-done.4.c_ref, ...), custom_call_target="tpu_custom_call", output_to_operand_aliasing={{}: (16, {})} | custom-call | tf_op jit(solution)/shard_map/last_blocks/pallas_call | solution.py:374
  (1 shorter events, 0.0 us)
Async XLA Ops:
  0.0 7.2 %collective-permute-start = (bf16[128,512]{1,0:T(8,128)(2,1)}, bf16[128,512]{1,0:T(8,128)(2,1)S(1)}, u32[]{:S(2)}, u32[]{:S(2)}) collective-permute-start(bf16[128,512]{1,0:T(8,128)(2,1)} %k_hbm.1), channel_id=1, source_target_pairs={{0,2},{1,3},{2,4},{3,5},{4,6},{5,7},{6,8},{7,9},{8,10},{9,11},{10,... | collective-permute-start | bytes 393224 | tf_op jit(solution)/shard_map/ppermute | solution.py:387
  1.2 7.3 %collective-permute-start.1 = (bf16[128,512]{1,0:T(8,128)(2,1)}, bf16[128,512]{1,0:T(8,128)(2,1)S(1)}, u32[]{:S(2)}, u32[]{:S(2)}) collective-permute-start(bf16[128,512]{1,0:T(8,128)(2,1)} %k_hbm.1), channel_id=1, source_target_pairs={{0,1},{1,0},{2,3},{3,2},{4,5},{5,4},{6,7},{7,6},{8,9},{9,8},{10,11... | collective-permute-start | bytes 393224 | tf_op jit(solution)/shard_map/ppermute | solution.py:387
  2.2 7.5 %collective-permute-start.2 = (bf16[128,512]{1,0:T(8,128)(2,1)}, bf16[128,512]{1,0:T(8,128)(2,1)S(1)}, u32[]{:S(2)}, u32[]{:S(2)}) collective-permute-start(bf16[128,512]{1,0:T(8,128)(2,1)} %v_hbm.1), channel_id=1, source_target_pairs={{0,2},{1,3},{2,4},{3,5},{4,6},{5,7},{6,8},{7,9},{8,10},{9,11},{10,... | collective-permute-start | bytes 393224 | tf_op jit(solution)/shard_map/ppermute | solution.py:387
  3.4 6.3 %collective-permute-start.3 = (bf16[128,512]{1,0:T(8,128)(2,1)}, bf16[128,512]{1,0:T(8,128)(2,1)S(1)}, u32[]{:S(2)}, u32[]{:S(2)}) collective-permute-start(bf16[128,512]{1,0:T(8,128)(2,1)} %v_hbm.1), channel_id=1, source_target_pairs={{0,1},{1,0},{2,3},{3,2},{4,5},{5,4},{6,7},{7,6},{8,9},{9,8},{10,11... | collective-permute-start | bytes 393224 | tf_op jit(solution)/shard_map/ppermute | solution.py:387
  5.7 8.4 %collective-permute-start.4 = (bf16[256,512]{1,0:T(8,128)(2,1)S(1)}, bf16[256,512]{1,0:T(8,128)(2,1)S(1)}, u32[]{:S(2)}, u32[]{:S(2)}) collective-permute-start(bf16[256,512]{1,0:T(8,128)(2,1)S(1)} %get-tuple-element.35.kv_ref), channel_id=1, source_target_pairs={{0,1},{1,4},{2,3},{3,6},{4,2},{5,8},{6,7},{7,10},{8,0},{9,12},{10,... | collective-permute-start | bytes 786440 | tf_op jit(solution)/shard_map/ppermute | solution.py:387
  7.2 4.4 %collective-permute-start.5 = (bf16[128,512]{1,0:T(8,128)(2,1)S(1)}, bf16[128,512]{1,0:T(8,128)(2,1)S(1)}, u32[]{:S(2)}, u32[]{:S(2)}) collective-permute-start(bf16[128,512]{1,0:T(8,128)(2,1)S(1)} %collective-permute-done.a_ref.ak_ref), channel_id=1, source_target_pairs={{0,1},{1,0},{2,3},{3,2},{4,5},{5,4},{6,7},{7,6},{8,9},{9,8},{10,11... | collective-permute-start | bytes 393224 | tf_op jit(solution)/shard_map/ppermute | solution.py:387
  11.1 1.5 %collective-permute-start.6 = (bf16[128,512]{1,0:T(8,128)(2,1)S(1)}, bf16[128,512]{1,0:T(8,128)(2,1)S(1)}, u32[]{:S(2)}, u32[]{:S(2)}) collective-permute-start(bf16[128,512]{1,0:T(8,128)(2,1)S(1)} %collective-permute-done.2.va_ref.av_ref), channel_id=1, source_target_pairs={{0,1},{1,0},{2,3},{3,2},{4,5},{5,4},{6,7},{7,6},{8,9},{9,8},{10,11... | collective-permute-start | bytes 393224 | tf_op jit(solution)/shard_map/ppermute | solution.py:387
